TPU v7x, 512 devices: a whole 4x8x8 slice. The times are simulated.
512 devices in a mesh: ri: 64 (over x, y_lo, z), bas: 8 (over y_hi, core).
Axes of the slice: x: 4, y: 8 (y_hi: 4, y_lo: 2; y = y_hi * 2 + y_lo), z: 8, core: 2. Of those that a mesh axis runs over, the one named last changes fastest.
Arguments:
- three_centre: bfloat16 [64, 8, 32, 2, 128, 128], P('ri', 'bas'), may hold values from -0.5 to 0.5
- slot_index: int32 [64, 8, 32, 3], P('ri', 'bas'), may hold values from 0 to 15, as said below
- slot_count: int32 [64, 8], P('ri', 'bas'), may hold values from 8 to 32, as said below
- panel_last: bfloat16 [2048, 512], P(('ri', 'bas')), may hold values from -0.125 to 0.125
- panel_prev: bfloat16 [2048, 512], P(('ri', 'bas')), may hold values from -0.125 to 0.125
- panel_older: bfloat16 [2048, 512], P(('ri', 'bas')), may hold values from -0.125 to 0.125
Outputs:
- exchange: float32 [8, 64, 4, 2048], P('bas', 'ri')
Inputs may be any that keep to these rules, and one draw needn't show every extreme that they name: `slot_index`: within one device the 32 slots name distinct triples; first column below 1, second below 2, third below 16. Slots from slot_count on are unused. `slot_count`: in every group of devices that share an ri index, one device uses all 32 slots.
All inputs are finite; a program needn't handle non-finite values.
Results may differ from a plain program's by a relative error of at most 0.0011.
Values may be sent and summed in bfloat16 or wider, within the bound.
A program may use at most 128 MiB of HBM per device.

v0:
```python
import jax
import jax.numpy as jnp
from jax import lax
from jax.sharding import PartitionSpec as P

BLK = 128
NBLK = 16
OCC = 512
RB = 2
P_DEV = 2


def assemble(blocks, slot_ids, live_count, orbital_panel, owned_blocks):
    slot_total = blocks.shape[0]
    group_size = 4
    panel_blocks = orbital_panel.reshape(NBLK, BLK, OCC)
    groups = P_DEV // RB * owned_blocks
    live_mask = jnp.arange(slot_total) < live_count
    segment = slot_ids[:, 0] * owned_blocks + slot_ids[:, 1]
    onehot = ((segment[:, None] == jnp.arange(groups)[None, :]) & live_mask[:, None]).astype(
        jnp.float32
    )
    steps_total = slot_total // group_size
    block_groups = blocks.reshape(steps_total, group_size, RB, BLK, BLK)
    column_groups = slot_ids[:, 2].reshape(steps_total, group_size)
    onehot_groups = onehot.reshape(steps_total, group_size, groups)

    def add_group(summed, item):
        group_blocks, group_columns, group_onehot = item
        chosen = panel_blocks[group_columns]
        slot_terms = jnp.einsum(
            "spmn,sni->spmi", group_blocks, chosen, preferred_element_type=jnp.float32
        )
        summed = summed + jnp.einsum(
            "sg,spmi->gpmi", group_onehot, slot_terms, precision=lax.Precision.HIGHEST
        )
        return (summed, None)

    start_sum = jnp.zeros((groups, RB, BLK, OCC), jnp.float32)
    summed, _ = lax.scan(add_group, start_sum, (block_groups, column_groups, onehot_groups))
    return summed.astype(jnp.bfloat16).reshape(P_DEV // RB, owned_blocks, RB, BLK, OCC)


def local(three_centre, slot_index, slot_count, panel_last, panel_prev, panel_older):
    predicted = (
        2.5 * panel_last.astype(jnp.float32)
        - 2.0 * panel_prev.astype(jnp.float32)
        + 0.5 * panel_older.astype(jnp.float32)
    ).astype(jnp.bfloat16)
    orbital_panel = lax.all_gather(predicted, ("ri", "bas"), axis=0, tiled=True)
    owned_blocks = NBLK // lax.axis_size("bas")
    row_width = owned_blocks * BLK
    own_half = assemble(
        three_centre[0, 0], slot_index[0, 0], slot_count[0, 0], orbital_panel, owned_blocks
    )
    product_block = jnp.einsum(
        "aupmi,avpli->umvl",
        own_half,
        lax.all_gather(own_half, "bas", axis=1, tiled=True),
        preferred_element_type=jnp.float32,
    )
    partial_sum = product_block.reshape(row_width, -1)
    summed = lax.psum(partial_sum, "ri")
    row_share = summed.shape[0] // lax.axis_size("ri")
    owned_rows = lax.dynamic_slice_in_dim(summed, lax.axis_index("ri") * row_share, row_share, 0)
    return (-0.25 * owned_rows)[None, None]


def solution(mesh):
    return jax.shard_map(
        local,
        mesh=mesh,
        in_specs=(
            P("ri", "bas", None, None, None, None),
            P("ri", "bas", None, None),
            P("ri", "bas"),
            P(("ri", "bas"), None),
            P(("ri", "bas"), None),
            P(("ri", "bas"), None),
        ),
        out_specs=P("bas", "ri", None, None),
        check_vma=False,
    )
```

profile of v0, /device:TPU:32, one launch (start us, length us, event | category | flops | bytes accessed | tf_op | source)
XLA Modules:
  0.0 1535.1 jit_solution(1297446598613487723)
XLA Ops:
  6.5 0.0 all-gather.7.cloned.1.call-start
  6.5 1.3 fusion.15
  7.9 0.0 all-gather.7.cloned.1.call-update
  7.9 0.0 all-gather.5.cloned.1.call-start
  7.9 0.7 copy.21
  8.7 0.1 eq.16
  9.4 0.1 reshape_squeeze.7
  9.5 761.4 %all-gather.7.cloned.1.call-done = bf16[512,4,512]{2,1,0:T(4,128)(2,1)} async-done(((bf16[1,4,512]{2,1,0:T(4,128)(2,1)}), bf16[512,4,512]{2,1,0:T(4,128)(2,1)}) %all-gather.7.cloned.1.call-update) | async-done | bytes 2097168 | tf_op jit(solution)/shard_map/all_gather | solution.py:50
  770.9 4.0 reshape.60
  774.9 79.0 %while.11 = (s32[]{:T(128)}, f32[2,2,128,512]{3,0,2,1:T(2,128)}, f32[8,4,2]{1,2,0:T(2,128)S(1)}, bf16[8,4,2,128,128]{4,3,2,1,0:T(8,128)(2,1)}, s32[8,4]{1,0:T(8,...) while((s32[]{:T(128)}, f32[2,2,128,512]{3,0,2,1:T(2,128)}, ...), condition=%wide.region_1.2_spmd.clone, body=%wide.region_0.1_spmd.clone.sunk | while | flops 147325968 | bytes 8132263 | solution.py:40
  774.9 2.2 gather_fusion
  777.1 1.4 fusion.30
  778.5 5.4 fusion.31
  783.9 2.2 gather_fusion
  786.1 1.4 fusion.30
  787.5 6.4 fusion.31
  793.9 2.2 gather_fusion
  796.1 1.4 fusion.30
  797.5 6.4 fusion.31
  803.9 2.2 gather_fusion
  806.1 1.4 fusion.30
  807.5 6.4 fusion.31
  813.9 2.2 gather_fusion
  816.1 1.4 fusion.30
  817.5 6.4 fusion.31
  823.9 2.2 gather_fusion
  826.1 1.4 fusion.30
  827.5 6.4 fusion.31
  833.9 2.2 gather_fusion
  836.1 1.4 fusion.30
  837.5 6.4 fusion.31
  843.9 2.2 gather_fusion
  846.1 1.4 fusion.30
  847.5 6.4 fusion.31
  853.9 2.2 copy.20
  856.1 0.0 all-gather.5.cloned.1.call-update
  856.1 0.0 all-reduce.2.cloned.1.call-start
  856.2 49.4 %all-gather.5.cloned.1.call-done = bf16[16,2,128,512]{3,2,0,1:T(8,128)(2,1)} async-done(((bf16[2,2,128,512]{3,2,0,1:T(8,128)(2,1)}), bf16[16,2,128,512]{3,2,0,1:T(8,128)(2,1)}) %all-gather.5.cloned.1.call-update) | async-done | bytes 4194320 | tf_op jit(solution)/shard_map/all_gather | solution.py:59
  905.6 5.0 convolution_bitcast_fusion
  910.5 0.0 all-reduce.2.cloned.1.call-update
  910.6 616.6 %all-reduce.2.cloned.1.call-done = f32[256,2048]{1,0:T(8,128)} async-done(((f32[256,2048]{1,0:T(8,128)}), f32[256,2048]{1,0:T(8,128)}) %all-reduce.2.cloned.1.call-update) | async-done | bytes 2097168 | tf_op jit(solution)/shard_map/psum | solution.py:63
  1527.1 1.5 multiply_bitcast_fusion
  (20 shorter events, 0.2 us)
Async XLA Ops:
  6.5 764.4 %all-gather.7.cloned.1.call-start = ((), (), s32[]{:S(2)}) async-start(), calls=%async_computation.2 | async-start | bytes 2101248 | tf_op jit(solution)/shard_map/all_gather | solution.py:50
  7.9 897.7 %all-gather.5.cloned.1.call-start = ((), (), s32[]{:S(2)}) async-start(), calls=%async_computation.1 | async-start | bytes 4718592 | tf_op jit(solution)/shard_map/all_gather | solution.py:59
  856.1 671.0 %all-reduce.2.cloned.1.call-start = ((), (), s32[]{:S(2)}) async-start(), calls=%async_computation | async-start | bytes 4194304 | tf_op jit(solution)/shard_map/psum | solution.py:63
Sparse Core Ops, SparseCore 0:
  9.5 761.4 all-gather.6
  856.2 49.2 all-gather.4
  910.7 616.4 all-reduce.1
where the time goes:
time: 1540 us
  waiting for transfers between devices  1430 us (93%)
  matrix products  66.3 us (4%)
  local copies, waits for them, and re-layouts  24.3 us (2%)
    all_gather x1, waiting for transfers between devices, local(): orbital_panel = lax.all_gather(predicted, ('ri', 'bas'), axis=0, tiled=True)  761 us
    psum x1, waiting for transfers between devices, local(): summed = lax.psum(partial_sum, 'ri')  617 us
    dot_general x8, matrix products, add_group(): jnp.einsum('sg,spmi->gpmi', group_onehot, slot_terms, precision=lax.Preci...  50.4 us
    all_gather x1, waiting for transfers between devices, local(): lax.all_gather(own_half, 'bas', axis=1, tiled=True)  49.4 us
  transfers between devices with their start and end apart: 3, of which 3 were waited for; matrix products, arithmetic and copies ran while one was open for 0% of the time, Pallas kernels for 0%

commit v1 on v0

v1 whole, which is shorter than its diff:
```python
import jax
import jax.numpy as jnp
from jax import lax
from jax.experimental import pallas as pl
from jax.experimental.pallas import tpu as pltpu
from jax.sharding import PartitionSpec as P

MESH = pl.DeviceIdType.MESH
BF16, F32 = jnp.bfloat16, jnp.float32

BLK = 128
NBLK = 16
OCC = 512
RB = 2
SLOTS = 32
ROWS = 256
NX, NYL, NZ, NYH, NC = 4, 2, 8, 4, 2
NRI = NX * NYL * NZ
NBAS = NYH * NC
NJ = 2
LW = OCC // NJ
XR = ROWS // NX
GW = 512


def kernel(
    inv_ref, live_ref, t_hbm, last_ref, prev_ref, older_ref, out_ref,
    t_v, dense, pred, heads, panel, half, part, sent, got, shareA, shareB, landA, landB,
    t_sem,
    s_head, r_head, s_z, r_z, s_xy, r_xy, s_core, r_core,
    s_y, r_y, s_hc, r_hc, s_x, r_x, s_fa, r_fa, s_fb, r_fb,
):
    ri, bas = lax.axis_index("ri"), lax.axis_index("bas")
    x, yl, z = ri // (NYL * NZ), (ri // NZ) % NYL, ri % NZ
    yh, core = bas // NC, bas % NC
    line = x * NYL + yl
    me = (ri, bas)
    other = (ri, yh * NC + 1 - core)

    def at(x_, yl_, z_):
        return (x_ * NYL + yl_) * NZ + z_

    def bas_peer(i):
        return (ri, (bas + i) % NBAS)

    def z_peer(i):
        return (at(x, yl, (z + i) % NZ), bas)

    def xy_peer(i):
        return (at((x + i // NYL) % NX, (yl + i % NYL) % NYL, z), bas)

    def yz_peer(i):
        return (at(x, (yl + i // NZ) % NYL, (z + i % NZ) % NZ), bas)

    def y_peer(i):
        return (ri, ((yh + i) % NYH) * NC + core)

    started = []

    def send(src, dst, ssem, rsem, dev):
        copy = pltpu.make_async_remote_copy(
            src_ref=src, dst_ref=dst, send_sem=ssem, recv_sem=rsem, device_id=dev, device_id_type=MESH
        )
        copy.start()
        started.append(copy)

    def arrive(dst, ssem, rsem):
        pltpu.make_async_remote_copy(
            src_ref=dst, dst_ref=dst, send_sem=ssem, recv_sem=rsem, device_id=other, device_id_type=MESH
        ).wait_recv()

    t_copy = pltpu.make_async_copy(t_hbm, t_v, t_sem)
    t_copy.start()

    peers = [bas_peer(i) for i in range(1, NBAS)]
    peers += [yz_peer(i) for i in range(1, NYL * NZ)]
    peers += [xy_peer(i) for i in range(NYL, NX * NYL)]
    barrier = pltpu.get_barrier_semaphore()
    for dev in peers:
        pl.semaphore_signal(barrier, inc=1, device_id=dev, device_id_type=MESH)

    mixed = (
        2.5 * last_ref[...].astype(F32) - 2.0 * prev_ref[...].astype(F32) + 0.5 * older_ref[...].astype(F32)
    ).astype(BF16)
    pred[...] = mixed.astype(F32)
    heads[bas] = mixed.astype(F32)
    pl.semaphore_wait(barrier, len(peers))

    for i in range(1, NBAS):
        send(pred, heads.at[bas], s_head.at[i], r_head.at[i], bas_peer(i))

    t_copy.wait()
    for u in range(ROWS // BLK):
        for v in range(NBLK):
            k = u * NBLK + v
            block = t_v[inv_ref[k]]
            block = jnp.where(live_ref[k] != 0, block, jnp.zeros_like(block))
            dense[:, pl.ds(u * BLK, BLK), pl.ds(v * BLK, BLK)] = block

    for i in range(1, NBAS):
        arrive(heads.at[(bas - i + NBAS) % NBAS], s_head.at[i], r_head.at[i])
    rows = jnp.concatenate([heads[core * 4 + i] for i in range(4)], axis=0).astype(BF16)
    for j in range(NJ):
        panel[j, ri, core] = rows[:, j * LW : (j + 1) * LW]

    mine = panel.at[:, ri, core]
    for i in range(1, NZ):
        send(mine, mine, s_z.at[i], r_z.at[i], z_peer(i))
    for i in range(1, NZ):
        src = at(x, yl, (z - i + NZ) % NZ)
        arrive(panel.at[:, src, core], s_z.at[i], r_z.at[i])

    for j in range(NJ):
        mine = panel.at[j, pl.ds(line * NZ, NZ), core]
        for i in range(1, NX * NYL):
            send(mine, mine, s_xy.at[j, i], r_xy.at[j, i], xy_peer(i))

    left, right = (yh - 1 + NYH) % NYH, (yh + 1) % NYH
    across = (yh + 2) % NYH

    def product(j, p):
        columns = panel[j].reshape(NBLK * BLK, LW)
        return jnp.dot(dense[p], columns, preferred_element_type=F32).astype(BF16)

    for j in range(NJ):
        for i in range(1, NX * NYL):
            src = ((x - i // NYL + NX) % NX) * NYL + (yl + i % NYL) % NYL
            arrive(panel.at[j, pl.ds(src * NZ, NZ), core], s_xy.at[j, i], r_xy.at[j, i])
        mine = panel.at[j, :, core]
        send(mine, mine, s_core.at[j], r_core.at[j], other)
        arrive(panel.at[j, :, 1 - core], s_core.at[j], r_core.at[j])
        for p in range(RB):
            half[bas, j, p] = product(j, p)
        mine = half.at[bas, j]
        send(mine, mine, s_y.at[j, 0], r_y.at[j, 0], y_peer(1))
        send(mine, mine, s_y.at[j, 1], r_y.at[j, 1], y_peer(3))
        send(mine, mine, s_hc.at[j, 0], r_hc.at[j, 0], other)

    def block(yh_):
        return half.at[yh_ * NC + core]

    def far_block(yh_):
        return half.at[yh_ * NC + 1 - core]

    def multiply(g, yh_):
        for c in range(NC):
            total = jnp.zeros((ROWS, ROWS), F32)
            for j in range(NJ):
                for p in range(RB):
                    total += lax.dot_general(
                        half[bas, j, p], half[yh_ * NC + c, j, p], (((1,), (1,)), ((), ())),
                        preferred_element_type=F32,
                    )
            part[g, :, c * ROWS : (c + 1) * ROWS] = total
            sent[g, :, c * ROWS : (c + 1) * ROWS] = total.astype(BF16)
        for i in range(1, NX):
            x_ = (x + i) % NX
            send(sent.at[g, pl.ds(x_ * XR, XR)], got.at[g, i], s_x.at[g, i], r_x.at[g, i], (at(x_, yl, z), bas))

    def sum_x(g):
        total = part[g, pl.ds(x * XR, XR), :]
        for i in range(1, NX):
            arrive(got.at[g, i], s_x.at[g, i], r_x.at[g, i])
        for i in range(1, NX):
            total += got[g, i].astype(F32)
        return total

    for j in range(NJ):
        arrive(far_block(yh).at[j], s_hc.at[j, 0], r_hc.at[j, 0])
    multiply(0, yh)

    for j in range(NJ):
        mine = block(left).at[j]
        arrive(mine, s_y.at[j, 0], r_y.at[j, 0])
        send(mine.at[0], mine.at[0], s_y.at[j, 2], r_y.at[j, 2], y_peer(1))
        send(mine, mine, s_hc.at[j, 1], r_hc.at[j, 1], other)
        mine = block(right).at[j]
        arrive(mine, s_y.at[j, 1], r_y.at[j, 1])
        send(mine.at[1], mine.at[1], s_y.at[j, 3], r_y.at[j, 3], y_peer(3))
        send(mine, mine, s_hc.at[j, 2], r_hc.at[j, 2], other)
    for g, yh_ in ((1, left), (2, right)):
        for j in range(NJ):
            arrive(far_block(yh_).at[j], s_hc.at[j, g], r_hc.at[j, g])
        multiply(g, yh_)

    here = yl * NZ + z
    for g in range(3):
        total = sum_x(g)
        for i in range(NYL * NZ):
            shareA[i, :, g * GW : (g + 1) * GW] = total[i * 4 : i * 4 + 4, :]
    landA[here] = shareA[here]
    for i in range(1, NYL * NZ):
        there = ((yl + i // NZ) % NYL) * NZ + (z + i % NZ) % NZ
        send(shareA.at[there], landA.at[here], s_fa.at[i], r_fa.at[i], yz_peer(i))

    for j in range(NJ):
        mine = block(across).at[j]
        arrive(mine.at[0], s_y.at[j, 2], r_y.at[j, 2])
        arrive(mine.at[1], s_y.at[j, 3], r_y.at[j, 3])
        send(mine, mine, s_hc.at[j, 3], r_hc.at[j, 3], other)
    for j in range(NJ):
        arrive(far_block(across).at[j], s_hc.at[j, 3], r_hc.at[j, 3])
    multiply(3, across)

    def came_from(i):
        return ((yl + i // NZ) % NYL) * NZ + (z - i % NZ + NZ) % NZ

    for i in range(1, NYL * NZ):
        arrive(landA.at[came_from(i)], s_fa.at[i], r_fa.at[i])
    total = landA[0]
    for i in range(1, NYL * NZ):
        total += landA[i]
    for g, yh_ in ((0, yh), (1, left), (2, right)):
        out_ref[:, pl.ds(pl.multiple_of(yh_ * GW, GW), GW)] = -0.25 * total[:, g * GW : (g + 1) * GW]

    total = sum_x(3)
    for i in range(NYL * NZ):
        shareB[i] = total[i * 4 : i * 4 + 4, :]
    landB[here] = shareB[here]
    for i in range(1, NYL * NZ):
        there = ((yl + i // NZ) % NYL) * NZ + (z + i % NZ) % NZ
        send(shareB.at[there], landB.at[here], s_fb.at[i], r_fb.at[i], yz_peer(i))
    for i in range(1, NYL * NZ):
        arrive(landB.at[came_from(i)], s_fb.at[i], r_fb.at[i])
    total = landB[0]
    for i in range(1, NYL * NZ):
        total += landB[i]
    out_ref[:, pl.ds(pl.multiple_of(across * GW, GW), GW)] = -0.25 * total

    for copy in started:
        copy.wait_send()


def local(three_centre, slot_index, slot_count, panel_last, panel_prev, panel_older):
    slots = slot_index[0, 0]
    key = slots[:, 1] * NBLK + slots[:, 2]
    ids = jnp.arange(SLOTS, dtype=jnp.int32)
    hit = key[None, :] == ids[:, None]
    inv = jnp.sum(jnp.where(hit, ids[None, :], 0), axis=1)
    live = jnp.sum(jnp.where(hit & (ids[None, :] < slot_count[0, 0]), 1, 0), axis=1)

    dma = pltpu.SemaphoreType.DMA
    smem, vmem = pl.BlockSpec(memory_space=pltpu.SMEM), pl.BlockSpec(memory_space=pltpu.VMEM)
    out = pl.pallas_call(
        kernel,
        out_shape=jax.ShapeDtypeStruct((4, NBLK * BLK), F32),
        in_specs=[smem, smem, pl.BlockSpec(memory_space=pl.ANY), vmem, vmem, vmem],
        out_specs=vmem,
        scratch_shapes=[
            pltpu.VMEM((SLOTS, RB, BLK, BLK), BF16),
            pltpu.VMEM((RB, ROWS, NBLK * BLK), BF16),
            pltpu.VMEM((4, OCC), F32),
            pltpu.VMEM((NBAS, 4, OCC), F32),
            pltpu.VMEM((NJ, NRI, 2, 16, LW), BF16),
            pltpu.VMEM((NBAS, NJ, RB, ROWS, LW), BF16),
            pltpu.VMEM((4, ROWS, GW), F32),
            pltpu.VMEM((4, ROWS, GW), BF16),
            pltpu.VMEM((4, NX, XR, GW), BF16),
            pltpu.VMEM((NYL * NZ, 4, 3 * GW), F32),
            pltpu.VMEM((NYL * NZ, 4, GW), F32),
            pltpu.VMEM((NYL * NZ, 4, 3 * GW), F32),
            pltpu.VMEM((NYL * NZ, 4, GW), F32),
            dma,
            dma((NBAS,)), dma((NBAS,)),
            dma((NZ,)), dma((NZ,)),
            dma((NJ, NX * NYL)), dma((NJ, NX * NYL)),
            dma((NJ,)), dma((NJ,)),
            dma((NJ, 4)), dma((NJ, 4)),
            dma((NJ, 4)), dma((NJ, 4)),
            dma((4, NX)), dma((4, NX)),
            dma((NYL * NZ,)), dma((NYL * NZ,)),
            dma((NYL * NZ,)), dma((NYL * NZ,)),
        ],
        compiler_params=pltpu.CompilerParams(
            collective_id=0, has_side_effects=True, vmem_limit_bytes=40 * 1024 * 1024
        ),
        cost_estimate=pl.CostEstimate(flops=2 << 30, bytes_accessed=3 << 20, transcendentals=0),
    )(inv, live, three_centre[0, 0], panel_last, panel_prev, panel_older)
    return out[None, None]


def solution(mesh):
    return jax.shard_map(
        local,
        mesh=mesh,
        in_specs=(
            P("ri", "bas", None, None, None, None),
            P("ri", "bas", None, None),
            P("ri", "bas"),
            P(("ri", "bas"), None),
            P(("ri", "bas"), None),
            P(("ri", "bas"), None),
        ),
        out_specs=P("bas", "ri", None, None),
        check_vma=False,
    )
```

time: 1540 us -> 104 us (0.07)
  the two profiles are of different devices: /device:TPU:32 before, /device:TPU:8 now
where the time goes in v1:
time: 104 us; the launch traced here: 103 us
  Pallas kernels  97.7 us (94%)
  local copies, waits for them, and re-layouts  4.95 us (5%)
    pallas_call x1, Pallas kernels, local(): pl.pallas_call(kernel, out_shape=jax.ShapeDtypeStruct((4, NBLK * BLK), F3...  97.7 us
    unnamed x10, local copies, waits for them, and re-layouts  4.95 us

profile of v1, /device:TPU:8, one launch (start us, length us, event | category | flops | bytes accessed | tf_op | source)
XLA Modules:
  0.0 103.5 jit_solution(12861002088825295011)
XLA Ops:
  0.7 0.7 copy.9
  1.4 0.1 select_reduce_fusion
  1.5 0.0 copy-start
  1.5 1.6 %copy-done = bf16[1,1,32,2,128,128]{5,4,3,2,1,0:T(8,128)(2,1)S(1)} copy-done((bf16[1,1,32,2,128,128]{5,4,3,2,1,0:T(8,128)(2,1)S(1)}, bf16[1,1,32,2,128,128]{5,4,3,2,1,0:T(8,128)(2,1)}, u32[]{:S(2)}) %copy-start) | copy-done | bytes 2097176
  3.1 0.0 copy-start.1
  3.1 0.7 copy-done.1
  3.8 0.0 copy-start.2
  3.8 0.7 copy-done.2
  4.4 0.0 copy-start.3
  4.4 0.7 copy-done.3
  5.1 97.7 %shard_map.64 = f32[4,2048]{1,0:T(4,128)S(1)} custom-call(s32[32]{0:T(128)S(1)} %get-tuple-element.6.inv_ref, s32[32]{0:T(128)S(1)} %get-tuple-element.5.live_ref, bf16[32,2,128,128]{3,2,1,0:T(8,128)(2,1)S(1)} %bitcast.10, bf16[4,512]{1,0:T(4,128)(2,1)S(1)} %copy-done.1, bf16[4,512]{1,0:T(4,128)(2,1)S(1)} %copy-done.2, bf16[4,512]{1,0:T(4,128)(2,1)S(1)} %copy-done.3), custom_call_target="tpu_custom_call" | custom-call | flops 2147483648 | bytes 3145728 | tf_op jit(solution)/shard_map/pallas_call | solution.py:244
  102.9 0.6 copy.12
  (2 shorter events, 0.0 us)
Async XLA Ops:
  1.5 1.6 %copy-start = (bf16[1,1,32,2,128,128]{5,4,3,2,1,0:T(8,128)(2,1)S(1)}, bf16[1,1,32,2,128,128]{5,4,3,2,1,0:T(8,128)(2,1)}, u32[]{:S(2)}) copy-start(bf16[1,1,32,2,128,128]{5,4,3,2,1,0:T(8,128)(2,1)} %param.6) | copy-start | bytes 6291460
  3.1 0.7 copy-start.1
  3.8 0.7 copy-start.2
  4.4 0.7 copy-start.3

commit v2 on v1

v2 whole, which is shorter than its diff:
```python
import jax
import jax.numpy as jnp
from jax import lax
from jax.experimental import pallas as pl
from jax.experimental.pallas import tpu as pltpu
from jax.sharding import PartitionSpec as P

MESH = pl.DeviceIdType.MESH
BF16, F32 = jnp.bfloat16, jnp.float32

BLK = 128
NBLK = 16
OCC = 512
RB = 2
SLOTS = 32
ROWS = 256
NX, NYL, NZ, NYH, NC = 4, 2, 8, 4, 2
NRI = NX * NYL * NZ
NBAS = NYH * NC
NJ = 4
LW = OCC // NJ
XR = ROWS // NX
GW = 512


def kernel(
    inv_ref, live_ref, t_hbm, mixed_ref, out_ref,
    t_v, dense, pred, heads, panel, half, part, sent, got, share, land, last, last_got,
    t_sem,
    s_head, r_head, s_z, r_z, s_pair, r_pair, s_line, r_line, s_core, r_core,
    s_y, r_y, s_hc, r_hc, s_x, r_x, s_f, r_f,
):
    ri, bas = lax.axis_index("ri"), lax.axis_index("bas")
    x, yl, z = ri // (NYL * NZ), (ri // NZ) % NYL, ri % NZ
    yh, core = bas // NC, bas % NC
    line = x * NYL + yl
    other = (ri, yh * NC + 1 - core)
    head_core = bas // 4
    head_slot = bas % 4

    def at(x_, yl_, z_):
        return (x_ * NYL + yl_) * NZ + z_

    def head_target(i):
        return (ri, ((yh + i) % NYH) * NC + head_core)

    def z_peer(i):
        return (at(x, yl, (z + i) % NZ), bas)

    def x_peer(i):
        return (at((x + i) % NX, yl, z), bas)

    def xy_peer(i):
        return (at((x + i // NYL) % NX, (yl + i % NYL) % NYL, z), bas)

    def y_peer(i):
        return (ri, ((yh + i) % NYH) * NC + core)

    pair = (at(x, 1 - yl, z), bas)
    started = []

    def remote(src, dst, ssem, rsem, dev):
        return pltpu.make_async_remote_copy(
            src_ref=src, dst_ref=dst, send_sem=ssem, recv_sem=rsem, device_id=dev, device_id_type=MESH
        )

    def send(src, dst, ssem, rsem, dev):
        copy = remote(src, dst, ssem, rsem, dev)
        copy.start()
        started.append(copy)

    def arrive(dst, ssem, rsem):
        remote(dst, dst, ssem, rsem, other).wait_recv()

    t_copy = pltpu.make_async_copy(t_hbm, t_v, t_sem)
    t_copy.start()

    barrier = pltpu.get_barrier_semaphore()

    peers = [(ri, (bas + i) % NBAS) for i in range(1, NBAS)]
    peers += [z_peer(i) for i in range(1, NZ)]
    peers += [xy_peer(i) for i in range(1, NX * NYL)]
    for dev in peers:
        pl.semaphore_signal(barrier, inc=1, device_id=dev, device_id_type=MESH)

    mixed = mixed_ref[...].astype(F32)
    packed = jnp.concatenate([mixed[:, j * LW : (j + 1) * LW] for j in range(NJ)], axis=0).astype(BF16)
    pred[...] = packed
    own_head = core == head_core

    @pl.when(own_head)
    def _():
        heads[head_slot] = packed

    pl.semaphore_wait(barrier, len(peers))

    def head_copy(i):
        return remote(pred, heads.at[head_slot], s_head.at[i], r_head.at[head_slot], head_target(i))

    for i in range(1, NYH):
        copy = head_copy(i)
        copy.start()
        started.append(copy)

    @pl.when(jnp.logical_not(own_head))
    def _():
        head_copy(0).start()

    t_copy.wait()
    for u in range(ROWS // BLK):
        for v in range(NBLK):
            k = u * NBLK + v
            block = t_v[inv_ref[k]]
            block = jnp.where(live_ref[k] != 0, block, jnp.zeros_like(block))
            for p in range(RB):
                dense[pl.ds(p * ROWS + u * BLK, BLK), pl.ds(v * BLK, BLK)] = block[p]

    for k in range(4):
        @pl.when(jnp.logical_not(own_head & (head_slot == k)))
        def _():
            arrive(heads.at[k], s_head.at[0], r_head.at[k])
    rows = [heads[k].astype(F32) for k in range(4)]
    for j in range(NJ):
        tile = jnp.concatenate([r[j * 4 : j * 4 + 4, :] for r in rows], axis=0)
        panel[j, ri, core] = tile.astype(BF16)

    mine = panel.at[:, ri, core]
    for i in range(1, NZ):
        send(mine, mine, s_z.at[i], r_z.at[i], z_peer(i))
    for i in range(1, NZ):
        src = at(x, yl, (z - i + NZ) % NZ)
        arrive(panel.at[:, src, core], s_z.at[i], r_z.at[i])

    def line_of(j, line_):
        return panel.at[j, pl.ds(line_ * NZ, NZ), core]

    pair_line = x * NYL + 1 - yl
    for j in range(NJ):
        mine = line_of(j, line)
        send(mine, mine, s_pair.at[j], r_pair.at[j], pair)

    def pass_own(j):
        mine = line_of(j, line)
        for i in range(1, NX):
            send(mine, mine, s_line.at[j, 0, i], r_line.at[j, 0, i], x_peer(i))

    def pass_pair(j):
        mine = line_of(j, pair_line)
        arrive(mine, s_pair.at[j], r_pair.at[j])
        for i in range(1, NX):
            send(mine, mine, s_line.at[j, 1, i], r_line.at[j, 1, i], x_peer(i))

    left, right = (yh - 1 + NYH) % NYH, (yh + 1) % NYH
    across = (yh + 2) % NYH

    pass_own(0)
    pass_pair(0)
    for j in range(NJ):
        for i in range(1, NX):
            x_ = (x - i + NX) % NX
            arrive(line_of(j, x_ * NYL + yl), s_line.at[j, 0, i], r_line.at[j, 0, i])
            arrive(line_of(j, x_ * NYL + 1 - yl), s_line.at[j, 1, i], r_line.at[j, 1, i])
        if j + 1 < NJ:
            pass_own(j + 1)
            pass_pair(j + 1)
        mine = panel.at[j, :, core]
        send(mine, mine, s_core.at[j], r_core.at[j], other)
        arrive(panel.at[j, :, 1 - core], s_core.at[j], r_core.at[j])
        columns = panel[j].reshape(NBLK * BLK, LW)
        rows = jnp.dot(dense[...], columns, preferred_element_type=F32).astype(BF16)
        for p in range(RB):
            half[bas, j, :, p * LW : (p + 1) * LW] = rows[p * ROWS : (p + 1) * ROWS, :]
        mine = half.at[bas, j]
        send(mine, mine, s_y.at[j, 0], r_y.at[j, 0], y_peer(1))
        send(mine, mine, s_y.at[j, 1], r_y.at[j, 1], y_peer(3))
        send(mine, mine, s_hc.at[j, 0], r_hc.at[j, 0], other)

    def block(yh_):
        return half.at[yh_ * NC + core]

    def far_block(yh_):
        return half.at[yh_ * NC + 1 - core]

    def multiply(g, yh_):
        for c in range(NC):
            total = jnp.zeros((ROWS, ROWS), F32)
            for j in range(NJ):
                total += lax.dot_general(
                    half[bas, j], half[yh_ * NC + c, j], (((1,), (1,)), ((), ())), preferred_element_type=F32
                )
            part[g, :, c * ROWS : (c + 1) * ROWS] = total
            sent[g, :, c * ROWS : (c + 1) * ROWS] = total.astype(BF16)

    def send_x(g):
        for i in range(1, NX):
            x_ = (x + i) % NX
            send(sent.at[g, pl.ds(x_ * XR, XR)], got.at[g, i], s_x.at[g, i], r_x.at[g, i], x_peer(i))

    def fold_x(g):
        for i in range(1, NX):
            arrive(got.at[g, i], s_x.at[g, i], r_x.at[g, i])
        total = part[g, pl.ds(x * XR, XR), :]
        for i in range(1, NX):
            total += got[g, i].astype(F32)
        for z_ in range(NZ):
            for yl_ in range(NYL):
                k = (yl_ * NZ + z_) * 4
                share[g, z_, yl_] = total[k : k + 4, :]
        land[g, z] = share[g, z]
        for i in range(1, NZ):
            send(share.at[g, (z + i) % NZ], land.at[g, z], s_f.at[g, i], r_f.at[g, i], z_peer(i))

    def fold_z(g):
        for i in range(1, NZ):
            arrive(land.at[g, (z - i + NZ) % NZ], s_f.at[g, i], r_f.at[g, i])
        for yl_ in range(NYL):
            total = land[g, 0, yl_]
            for z_ in range(1, NZ):
                total += land[g, z_, yl_]
            last[g, yl_] = total
        send(last.at[g, 1 - yl], last_got.at[g], s_f.at[g, 0], r_f.at[g, 0], pair)

    def finish(g, yh_):
        arrive(last_got.at[g], s_f.at[g, 0], r_f.at[g, 0])
        out_ref[:, pl.ds(pl.multiple_of(yh_ * GW, GW), GW)] = -0.25 * (last[g, yl] + last_got[g])

    for j in range(NJ):
        arrive(far_block(yh).at[j], s_hc.at[j, 0], r_hc.at[j, 0])
    multiply(0, yh)
    send_x(0)

    def forward(j):
        if j % 2 == 0:
            mine = block(left).at[j]
            send(mine, mine, s_y.at[j, 2], r_y.at[j, 2], y_peer(1))
        else:
            mine = block(right).at[j]
            send(mine, mine, s_y.at[j, 2], r_y.at[j, 2], y_peer(3))

    for j in range(NJ):
        mine = block(left).at[j]
        arrive(mine, s_y.at[j, 0], r_y.at[j, 0])
        send(mine, mine, s_hc.at[j, 1], r_hc.at[j, 1], other)
        mine = block(right).at[j]
        arrive(mine, s_y.at[j, 1], r_y.at[j, 1])
        send(mine, mine, s_hc.at[j, 2], r_hc.at[j, 2], other)
        if j == 0:
            fold_x(0)
        if j == NJ - 2:
            forward(0)
            forward(1)
    for j in range(2, NJ):
        forward(j)
    for g, yh_ in ((1, left), (2, right)):
        for j in range(NJ):
            arrive(far_block(yh_).at[j], s_hc.at[j, g], r_hc.at[j, g])
        multiply(g, yh_)
        send_x(g)
    fold_x(1)
    fold_x(2)

    for j in range(NJ):
        mine = block(across).at[j]
        arrive(mine, s_y.at[j, 2], r_y.at[j, 2])
        send(mine, mine, s_hc.at[j, 3], r_hc.at[j, 3], other)
    for j in range(NJ):
        arrive(far_block(across).at[j], s_hc.at[j, 3], r_hc.at[j, 3])
    multiply(3, across)

    for i in range(1, NX * NYL):
        line_ = ((x + i // NYL) % NX) * NYL + (yl + i % NYL) % NYL
        src = sent.at[3, pl.ds(line_ * 32, 32)]
        dst = got.at[3, i // NYL, pl.ds((i % NYL) * 32, 32)]
        send(src, dst, s_f.at[3, i], r_f.at[3, i], xy_peer(i))
    for g in range(3):
        fold_z(g)
    for i in range(1, NX * NYL):
        arrive(got.at[3, i // NYL, pl.ds((i % NYL) * 32, 32)], s_f.at[3, i], r_f.at[3, i])
    total = part[3, pl.ds(line * 32, 32), :]
    for i in range(1, NX * NYL):
        total += got[3, i // NYL, (i % NYL) * 32 : (i % NYL) * 32 + 32, :].astype(F32)
    for i in range(NZ):
        share[3, i, 0] = total[i * 4 : i * 4 + 4, :]
    land[3, z, 0] = share[3, z, 0]
    for i in range(1, NZ):
        src, dst = share.at[3, (z + i) % NZ, 0], land.at[3, z, 0]
        send(src, dst, s_f.at[3, NX * NYL + i], r_f.at[3, NX * NYL + i], z_peer(i))
    finish(0, yh)
    finish(1, left)
    finish(2, right)
    for i in range(1, NZ):
        arrive(land.at[3, (z - i + NZ) % NZ, 0], s_f.at[3, NX * NYL + i], r_f.at[3, NX * NYL + i])
    total = land[3, 0, 0]
    for i in range(1, NZ):
        total += land[3, i, 0]
    out_ref[:, pl.ds(pl.multiple_of(across * GW, GW), GW)] = -0.25 * total

    for copy in started:
        copy.wait_send()

    @pl.when(jnp.logical_not(own_head))
    def _():
        head_copy(0).wait_send()


def local(three_centre, slot_index, slot_count, panel_last, panel_prev, panel_older):
    mixed = (
        2.5 * panel_last.astype(F32) - 2.0 * panel_prev.astype(F32) + 0.5 * panel_older.astype(F32)
    ).astype(BF16)
    slots = slot_index[0, 0]
    key = slots[:, 1] * NBLK + slots[:, 2]
    ids = jnp.arange(SLOTS, dtype=jnp.int32)
    hit = key[None, :] == ids[:, None]
    inv = jnp.sum(jnp.where(hit, ids[None, :], 0), axis=1)
    live = jnp.sum(jnp.where(hit & (ids[None, :] < slot_count[0, 0]), 1, 0), axis=1)

    dma = pltpu.SemaphoreType.DMA
    smem, vmem = pl.BlockSpec(memory_space=pltpu.SMEM), pl.BlockSpec(memory_space=pltpu.VMEM)
    out = pl.pallas_call(
        kernel,
        out_shape=jax.ShapeDtypeStruct((4, NBLK * BLK), F32),
        in_specs=[smem, smem, pl.BlockSpec(memory_space=pl.ANY), vmem],
        out_specs=vmem,
        scratch_shapes=[
            pltpu.VMEM((SLOTS, RB, BLK, BLK), BF16),
            pltpu.VMEM((RB * ROWS, NBLK * BLK), BF16),
            pltpu.VMEM((16, BLK), BF16),
            pltpu.VMEM((4, 16, BLK), BF16),
            pltpu.VMEM((NJ, NRI, 2, 16, LW), BF16),
            pltpu.VMEM((NBAS, NJ, ROWS, RB * LW), BF16),
            pltpu.VMEM((4, ROWS, GW), F32),
            pltpu.VMEM((4, ROWS, GW), BF16),
            pltpu.VMEM((4, NX, XR, GW), BF16),
            pltpu.VMEM((4, NZ, NYL, 4, GW), F32),
            pltpu.VMEM((4, NZ, NYL, 4, GW), F32),
            pltpu.VMEM((3, NYL, 4, GW), F32),
            pltpu.VMEM((3, 4, GW), F32),
            dma,
            dma((NYH,)), dma((4,)),
            dma((NZ,)), dma((NZ,)),
            dma((NJ,)), dma((NJ,)),
            dma((NJ, NYL, NX)), dma((NJ, NYL, NX)),
            dma((NJ,)), dma((NJ,)),
            dma((NJ, 3)), dma((NJ, 3)),
            dma((NJ, 4)), dma((NJ, 4)),
            dma((3, NX)), dma((3, NX)),
            dma((4, NYL * NZ)), dma((4, NYL * NZ)),
        ],
        compiler_params=pltpu.CompilerParams(
            collective_id=0, has_side_effects=True, vmem_limit_bytes=53 * 1024 * 1024
        ),
        cost_estimate=pl.CostEstimate(flops=2 << 30, bytes_accessed=3 << 20, transcendentals=0),
    )(inv, live, three_centre[0, 0], mixed)
    return out[None, None]


def solution(mesh):
    return jax.shard_map(
        local,
        mesh=mesh,
        in_specs=(
            P("ri", "bas", None, None, None, None),
            P("ri", "bas", None, None),
            P("ri", "bas"),
            P(("ri", "bas"), None),
            P(("ri", "bas"), None),
            P(("ri", "bas"), None),
        ),
        out_specs=P("bas", "ri", None, None),
        check_vma=False,
    )
```

time: 104 us -> 89.7 us (0.86)
  the two profiles are of different devices: /device:TPU:8 before, /device:TPU:1 now
where the time goes in v2:
time: 89.7 us; the launch traced here: 89.6 us
  Pallas kernels  86.7 us (97%)
  local copies, waits for them, and re-layouts  1.3 us (1%)
    pallas_call x1, Pallas kernels, local(): pl.pallas_call(kernel, out_shape=jax.ShapeDtypeStruct((4, NBLK * BLK), F3...  86.7 us

profile of v2, /device:TPU:1, one launch (start us, length us, event | category | flops | bytes accessed | tf_op | source)
XLA Modules:
  0.0 89.6 jit_solution(926696832270801190)
XLA Ops:
  0.7 0.7 copy.9
  1.4 0.1 select_reduce_fusion
  1.5 0.7 add_convert_fusion.mixed_ref
  2.2 86.7 %shard_map.64 = f32[4,2048]{1,0:T(4,128)S(1)} custom-call(s32[32]{0:T(128)S(1)} %get-tuple-element.6.inv_ref, s32[32]{0:T(128)S(1)} %get-tuple-element.5.live_ref, bf16[32,2,128,128]{3,2,1,0:T(8,128)(2,1)} %bitcast.11, bf16[4,512]{1,0:T(4,128)(2,1)S(1)} %add_convert_fusion.mixed_ref), custom_call_target="tpu_custom_call" | custom-call | flops 2147483648 | bytes 3145728 | tf_op jit(solution)/shard_map/pallas_call | solution.py:319
  88.9 0.6 copy.12
  (2 shorter events, 0.0 us)

commit v3 on v2

--- a/solution.py
+++ b/solution.py
@@ -24,11 +24,11 @@
 
 
 def kernel(
-    inv_ref, live_ref, t_hbm, mixed_ref, out_ref,
-    t_v, dense, pred, heads, panel, half, part, sent, got, share, land, last, last_got,
-    t_sem,
-    s_head, r_head, s_z, r_z, s_pair, r_pair, s_line, r_line, s_core, r_core,
-    s_y, r_y, s_hc, r_hc, s_x, r_x, s_f, r_f,
+    t_hbm, slots_hbm, count_hbm, last_hbm, prev_hbm, older_hbm, out_ref,
+    t_v, slots_v, count_v, panels_v, table_v, table, dense, pred, heads, panel, half, part, sent, got, share, land, last, last_got,
+    in_sem,
+    s_head, r_head, s_z, r_z, s_xy, r_xy, s_lc, r_lc, s_pair, r_pair, s_line, r_line, s_core, r_core,
+    s_y, r_y, s_hc, r_hc, s_x, r_x, s_f, r_f, s_last, r_last,
 ):
     ri, bas = lax.axis_index("ri"), lax.axis_index("bas")
     x, yl, z = ri // (NYL * NZ), (ri // NZ) % NYL, ri % NZ
@@ -72,8 +72,15 @@
     def arrive(dst, ssem, rsem):
         remote(dst, dst, ssem, rsem, other).wait_recv()
 
-    t_copy = pltpu.make_async_copy(t_hbm, t_v, t_sem)
-    t_copy.start()
+    loads = [
+        pltpu.make_async_copy(src, dst, in_sem.at[i])
+        for i, (src, dst) in enumerate((
+            (last_hbm, panels_v.at[0]), (prev_hbm, panels_v.at[1]), (older_hbm, panels_v.at[2]),
+            (slots_hbm, slots_v), (count_hbm, count_v), (t_hbm, t_v),
+        ))
+    ]
+    for copy in loads:
+        copy.start()
 
     barrier = pltpu.get_barrier_semaphore()
 
@@ -83,7 +90,10 @@
     for dev in peers:
         pl.semaphore_signal(barrier, inc=1, device_id=dev, device_id_type=MESH)
 
-    mixed = mixed_ref[...].astype(F32)
+    for copy in loads[:3]:
+        copy.wait()
+    panels = [panels_v[i].astype(F32) for i in range(3)]
+    mixed = 2.5 * panels[0] - 2.0 * panels[1] + 0.5 * panels[2]
     packed = jnp.concatenate([mixed[:, j * LW : (j + 1) * LW] for j in range(NJ)], axis=0).astype(BF16)
     pred[...] = packed
     own_head = core == head_core
@@ -106,12 +116,25 @@
     def _():
         head_copy(0).start()
 
-    t_copy.wait()
+    loads[3].wait()
+    loads[4].wait()
+    key = slots_v[0, 1] * NBLK + slots_v[0, 2]
+    slot = lax.broadcasted_iota(jnp.int32, (SLOTS, SLOTS), 1)
+    hit = lax.broadcasted_iota(jnp.int32, (SLOTS, SLOTS), 0) == key
+    used = hit & (slot < count_v[...])
+    inv = jnp.max(jnp.where(hit, slot, 0), axis=1, keepdims=True)
+    live = jnp.sum(jnp.where(used, 1, 0), axis=1, keepdims=True)
+    table_v[0] = jnp.broadcast_to(inv, (SLOTS, BLK))
+    table_v[1] = jnp.broadcast_to(live, (SLOTS, BLK))
+    copy = pltpu.make_async_copy(table_v, table, in_sem.at[6])
+    copy.start()
+    copy.wait()
+    loads[5].wait()
     for u in range(ROWS // BLK):
         for v in range(NBLK):
             k = u * NBLK + v
-            block = t_v[inv_ref[k]]
-            block = jnp.where(live_ref[k] != 0, block, jnp.zeros_like(block))
+            block = t_v[table[0, k, 0]]
+            block = jnp.where(table[1, k, 0] != 0, block, jnp.zeros_like(block))
             for p in range(RB):
                 dense[pl.ds(p * ROWS + u * BLK, BLK), pl.ds(v * BLK, BLK)] = block[p]
 
@@ -135,7 +158,15 @@
         return panel.at[j, pl.ds(line_ * NZ, NZ), core]
 
     pair_line = x * NYL + 1 - yl
-    for j in range(NJ):
+    def pass_core(line_):
+        mine = line_of(0, line_)
+        send(mine, mine, s_lc.at[line_], r_lc.at[line_], other)
+
+    mine = line_of(0, line)
+    for i in range(1, NX * NYL):
+        send(mine, mine, s_xy.at[i], r_xy.at[i], xy_peer(i))
+    pass_core(line)
+    for j in range(1, NJ):
         mine = line_of(j, line)
         send(mine, mine, s_pair.at[j], r_pair.at[j], pair)
 
@@ -153,19 +184,27 @@
     left, right = (yh - 1 + NYH) % NYH, (yh + 1) % NYH
     across = (yh + 2) % NYH
 
-    pass_own(0)
-    pass_pair(0)
     for j in range(NJ):
-        for i in range(1, NX):
-            x_ = (x - i + NX) % NX
-            arrive(line_of(j, x_ * NYL + yl), s_line.at[j, 0, i], r_line.at[j, 0, i])
-            arrive(line_of(j, x_ * NYL + 1 - yl), s_line.at[j, 1, i], r_line.at[j, 1, i])
-        if j + 1 < NJ:
-            pass_own(j + 1)
-            pass_pair(j + 1)
-        mine = panel.at[j, :, core]
-        send(mine, mine, s_core.at[j], r_core.at[j], other)
-        arrive(panel.at[j, :, 1 - core], s_core.at[j], r_core.at[j])
+        if j == 0:
+            for i in (1, 2, 6, 3, 7, 4, 5):
+                line_ = ((x - i // NYL + NX) % NX) * NYL + (yl + i % NYL) % NYL
+                arrive(line_of(0, line_), s_xy.at[i], r_xy.at[i])
+                pass_core(line_)
+                if i == 6:
+                    pass_own(1)
+            pass_pair(1)
+        else:
+            for i in range(1, NX):
+                x_ = (x - i + NX) % NX
+                arrive(line_of(j, x_ * NYL + yl), s_line.at[j, 0, i], r_line.at[j, 0, i])
+                arrive(line_of(j, x_ * NYL + 1 - yl), s_line.at[j, 1, i], r_line.at[j, 1, i])
+        if j == 0:
+            for line_ in range(NX * NYL):
+                arrive(panel.at[0, pl.ds(line_ * NZ, NZ), 1 - core], s_lc.at[line_], r_lc.at[line_])
+        else:
+            mine = panel.at[j, :, core]
+            send(mine, mine, s_core.at[j], r_core.at[j], other)
+            arrive(panel.at[j, :, 1 - core], s_core.at[j], r_core.at[j])
         columns = panel[j].reshape(NBLK * BLK, LW)
         rows = jnp.dot(dense[...], columns, preferred_element_type=F32).astype(BF16)
         for p in range(RB):
@@ -174,6 +213,9 @@
         send(mine, mine, s_y.at[j, 0], r_y.at[j, 0], y_peer(1))
         send(mine, mine, s_y.at[j, 1], r_y.at[j, 1], y_peer(3))
         send(mine, mine, s_hc.at[j, 0], r_hc.at[j, 0], other)
+        if j + 2 < NJ:
+            pass_own(j + 2)
+            pass_pair(j + 2)
 
     def block(yh_):
         return half.at[yh_ * NC + core]
@@ -181,15 +223,16 @@
     def far_block(yh_):
         return half.at[yh_ * NC + 1 - core]
 
-    def multiply(g, yh_):
-        for c in range(NC):
-            total = jnp.zeros((ROWS, ROWS), F32)
-            for j in range(NJ):
-                total += lax.dot_general(
-                    half[bas, j], half[yh_ * NC + c, j], (((1,), (1,)), ((), ())), preferred_element_type=F32
-                )
-            part[g, :, c * ROWS : (c + 1) * ROWS] = total
-            sent[g, :, c * ROWS : (c + 1) * ROWS] = total.astype(BF16)
+    def multiply(g, yh_, c, chunks, first=True, last=True):
+        cols = pl.ds(pl.multiple_of(c * ROWS, ROWS), ROWS)
+        total = jnp.zeros((ROWS, ROWS), F32) if first else part[g, :, cols]
+        for j in chunks:
+            total += lax.dot_general(
+                half[bas, j], half[yh_ * NC + c, j], (((1,), (1,)), ((), ())), preferred_element_type=F32
+            )
+        part[g, :, cols] = total
+        if last:
+            sent[g, :, cols] = total.astype(BF16)
 
     def send_x(g):
         for i in range(1, NX):
@@ -226,7 +269,8 @@
 
     for j in range(NJ):
         arrive(far_block(yh).at[j], s_hc.at[j, 0], r_hc.at[j, 0])
-    multiply(0, yh)
+    for c in range(NC):
+        multiply(0, yh, c, range(NJ))
     send_x(0)
 
     def forward(j):
@@ -254,28 +298,46 @@
     for g, yh_ in ((1, left), (2, right)):
         for j in range(NJ):
             arrive(far_block(yh_).at[j], s_hc.at[j, g], r_hc.at[j, g])
-        multiply(g, yh_)
+        for c in range(NC):
+            multiply(g, yh_, c, range(NJ))
         send_x(g)
+    def far(chunks):
+        for j in chunks:
+            mine = block(across).at[j]
+            arrive(mine, s_y.at[j, 2], r_y.at[j, 2])
+            send(mine, mine, s_hc.at[j, 3], r_hc.at[j, 3], other)
+
+    def far_other(chunks):
+        for j in chunks:
+            arrive(far_block(across).at[j], s_hc.at[j, 3], r_hc.at[j, 3])
+
+    def last_parts(i, c):
+        cols = pl.ds(pl.multiple_of(c * ROWS, ROWS), ROWS)
+        return got.at[3, i // NYL, pl.ds((i % NYL) * 32, 32), cols], cols
+
+    def send_last(k, c):
+        for i in range(1, NX * NYL):
+            line_ = ((x + i // NYL) % NX) * NYL + (yl + i % NYL) % NYL
+            dst, cols = last_parts(i, c)
+            send(sent.at[3, pl.ds(line_ * 32, 32), cols], dst, s_last.at[k, i], r_last.at[k, i], xy_peer(i))
+
+    far((0, 1))
     fold_x(1)
+    far_other((0, 1))
+    for c in range(NC):
+        multiply(3, across, c, (0, 1), True, False)
     fold_x(2)
-
-    for j in range(NJ):
-        mine = block(across).at[j]
-        arrive(mine, s_y.at[j, 2], r_y.at[j, 2])
-        send(mine, mine, s_hc.at[j, 3], r_hc.at[j, 3], other)
-    for j in range(NJ):
-        arrive(far_block(across).at[j], s_hc.at[j, 3], r_hc.at[j, 3])
-    multiply(3, across)
-
-    for i in range(1, NX * NYL):
-        line_ = ((x + i // NYL) % NX) * NYL + (yl + i % NYL) % NYL
-        src = sent.at[3, pl.ds(line_ * 32, 32)]
-        dst = got.at[3, i // NYL, pl.ds((i % NYL) * 32, 32)]
-        send(src, dst, s_f.at[3, i], r_f.at[3, i], xy_peer(i))
+    far((2, 3))
+    multiply(3, across, core, (2, 3), False, True)
+    send_last(0, core)
+    far_other((2, 3))
+    multiply(3, across, 1 - core, (2, 3), False, True)
+    send_last(1, 1 - core)
     for g in range(3):
         fold_z(g)
-    for i in range(1, NX * NYL):
-        arrive(got.at[3, i // NYL, pl.ds((i % NYL) * 32, 32)], s_f.at[3, i], r_f.at[3, i])
+    for k, c in ((0, core), (1, 1 - core)):
+        for i in range(1, NX * NYL):
+            arrive(last_parts(i, c)[0], s_last.at[k, i], r_last.at[k, i])
     total = part[3, pl.ds(line * 32, 32), :]
     for i in range(1, NX * NYL):
         total += got[3, i // NYL, (i % NYL) * 32 : (i % NYL) * 32 + 32, :].astype(F32)
@@ -284,12 +346,12 @@
     land[3, z, 0] = share[3, z, 0]
     for i in range(1, NZ):
         src, dst = share.at[3, (z + i) % NZ, 0], land.at[3, z, 0]
-        send(src, dst, s_f.at[3, NX * NYL + i], r_f.at[3, NX * NYL + i], z_peer(i))
+        send(src, dst, s_f.at[3, i], r_f.at[3, i], z_peer(i))
     finish(0, yh)
     finish(1, left)
     finish(2, right)
     for i in range(1, NZ):
-        arrive(land.at[3, (z - i + NZ) % NZ, 0], s_f.at[3, NX * NYL + i], r_f.at[3, NX * NYL + i])
+        arrive(land.at[3, (z - i + NZ) % NZ, 0], s_f.at[3, i], r_f.at[3, i])
     total = land[3, 0, 0]
     for i in range(1, NZ):
         total += land[3, i, 0]
@@ -304,25 +366,21 @@
 
 
 def local(three_centre, slot_index, slot_count, panel_last, panel_prev, panel_older):
-    mixed = (
-        2.5 * panel_last.astype(F32) - 2.0 * panel_prev.astype(F32) + 0.5 * panel_older.astype(F32)
-    ).astype(BF16)
-    slots = slot_index[0, 0]
-    key = slots[:, 1] * NBLK + slots[:, 2]
-    ids = jnp.arange(SLOTS, dtype=jnp.int32)
-    hit = key[None, :] == ids[:, None]
-    inv = jnp.sum(jnp.where(hit, ids[None, :], 0), axis=1)
-    live = jnp.sum(jnp.where(hit & (ids[None, :] < slot_count[0, 0]), 1, 0), axis=1)
-
+    slots = jnp.transpose(slot_index, (0, 3, 1, 2))
     dma = pltpu.SemaphoreType.DMA
-    smem, vmem = pl.BlockSpec(memory_space=pltpu.SMEM), pl.BlockSpec(memory_space=pltpu.VMEM)
+    hbm, vmem = pl.BlockSpec(memory_space=pltpu.HBM), pl.BlockSpec(memory_space=pltpu.VMEM)
     out = pl.pallas_call(
         kernel,
         out_shape=jax.ShapeDtypeStruct((4, NBLK * BLK), F32),
-        in_specs=[smem, smem, pl.BlockSpec(memory_space=pl.ANY), vmem],
+        in_specs=[hbm] * 6,
         out_specs=vmem,
         scratch_shapes=[
             pltpu.VMEM((SLOTS, RB, BLK, BLK), BF16),
+            pltpu.VMEM((1, 3, 1, SLOTS), jnp.int32),
+            pltpu.VMEM((1, 1), jnp.int32),
+            pltpu.VMEM((3, 4, OCC), BF16),
+            pltpu.VMEM((2, SLOTS, BLK), jnp.int32),
+            pltpu.SMEM((2, SLOTS, BLK), jnp.int32),
             pltpu.VMEM((RB * ROWS, NBLK * BLK), BF16),
             pltpu.VMEM((16, BLK), BF16),
             pltpu.VMEM((4, 16, BLK), BF16),
@@ -335,22 +393,25 @@
             pltpu.VMEM((4, NZ, NYL, 4, GW), F32),
             pltpu.VMEM((3, NYL, 4, GW), F32),
             pltpu.VMEM((3, 4, GW), F32),
-            dma,
+            dma((7,)),
             dma((NYH,)), dma((4,)),
             dma((NZ,)), dma((NZ,)),
+            dma((NX * NYL,)), dma((NX * NYL,)),
+            dma((NX * NYL,)), dma((NX * NYL,)),
             dma((NJ,)), dma((NJ,)),
             dma((NJ, NYL, NX)), dma((NJ, NYL, NX)),
             dma((NJ,)), dma((NJ,)),
             dma((NJ, 3)), dma((NJ, 3)),
             dma((NJ, 4)), dma((NJ, 4)),
             dma((3, NX)), dma((3, NX)),
-            dma((4, NYL * NZ)), dma((4, NYL * NZ)),
+            dma((4, NZ)), dma((4, NZ)),
+            dma((NC, NX * NYL)), dma((NC, NX * NYL)),
         ],
         compiler_params=pltpu.CompilerParams(
-            collective_id=0, has_side_effects=True, vmem_limit_bytes=53 * 1024 * 1024
+            collective_id=0, has_side_effects=True, vmem_limit_bytes=60 * 1024 * 1024
         ),
         cost_estimate=pl.CostEstimate(flops=2 << 30, bytes_accessed=3 << 20, transcendentals=0),
-    )(inv, live, three_centre[0, 0], mixed)
+    )(three_centre[0, 0], slots, slot_count, panel_last, panel_prev, panel_older)
     return out[None, None]
 
 

time: 89.7 us -> 88 us (0.981)
  Pallas kernels: 86.7 us -> 85.7 us
    pallas_call x1, Pallas kernels: 86.7 us -> 85.7 us  [local(): pl.pallas_call(kernel, out_shape=jax.ShapeDtypeStruct((4, NBLK * BLK), F3...]
where the time goes in v3:
time: 88 us; the launch traced here: 87.8 us
  Pallas kernels  85.7 us (97%)
  local copies, waits for them, and re-layouts  1.38 us (2%)
    pallas_call x1, Pallas kernels, local(): pl.pallas_call(kernel, out_shape=jax.ShapeDtypeStruct((4, NBLK * BLK), F3...  85.7 us

profile of v3, /device:TPU:1, one launch (start us, length us, event | category | flops | bytes accessed | tf_op | source)
XLA Modules:
  0.0 87.8 jit_solution(1461030659265626813)
XLA Ops:
  0.7 85.7 %shard_map.64 = f32[4,2048]{1,0:T(4,128)} custom-call(bf16[32,2,128,128]{3,2,1,0:T(8,128)(2,1)} %bitcast.4, s32[1,3,1,32]{3,2,1,0:T(1,128)} %bitcast.5, s32[1,1]{1,0:T(1,128)S(6)} %copy.8.count_hbm, bf16[4,512]{1,0:T(4,128)(2,1)} %last_hbm.1, bf16[4,512]{1,0:T(4,128)(2,1)} %prev_hbm.1, bf16[4,512]{1,0:T(4,128)(2,1)} %older_hbm.1), custom_call_target="tpu_custom_call" | custom-call | flops 2147483648 | bytes 3145728 | tf_op jit(solution)/shard_map/pallas_call | solution.py:372
  86.4 1.4 %copy.9 = f32[1,1,4,2048]{3,2,1,0:T(4,128)} copy(f32[1,1,4,2048]{3,2,1,0:T(4,128)} %bitcast.3) | data formatting | bytes 65536

commit v4 on v3

--- a/solution.py
+++ b/solution.py
@@ -25,10 +25,11 @@
 
 def kernel(
     t_hbm, slots_hbm, count_hbm, last_hbm, prev_hbm, older_hbm, out_ref,
-    t_v, slots_v, count_v, panels_v, table_v, table, dense, pred, heads, panel, half, part, sent, got, share, land, last, last_got,
+    t_v, slots_v, count_v, panels_v, table_v, table, dense, pred, heads, panel, half, near, far,
+    part, sent, got, share, land, last, fin,
     in_sem,
     s_head, r_head, s_z, r_z, s_xy, r_xy, s_lc, r_lc, s_pair, r_pair, s_line, r_line, s_core, r_core,
-    s_y, r_y, s_hc, r_hc, s_x, r_x, s_f, r_f, s_last, r_last,
+    s_y, r_y, s_hc, r_hc, s_x, r_x, s_f, r_f, s_fin, r_fin,
 ):
     ri, bas = lax.axis_index("ri"), lax.axis_index("bas")
     x, yl, z = ri // (NYL * NZ), (ri // NZ) % NYL, ri % NZ
@@ -53,8 +54,11 @@
     def xy_peer(i):
         return (at((x + i // NYL) % NX, (yl + i % NYL) % NYL, z), bas)
 
-    def y_peer(i):
-        return (ri, ((yh + i) % NYH) * NC + core)
+    y = yh * NYL + yl
+
+    def y_chip(d):
+        y_ = (y + d + NYL * NYH) % (NYL * NYH)
+        return (at(x, y_ % NYL, z), (y_ // NYL) * NC + core)
 
     pair = (at(x, 1 - yl, z), bas)
     started = []
@@ -68,6 +72,10 @@
         copy = remote(src, dst, ssem, rsem, dev)
         copy.start()
         started.append(copy)
+
+    def drain(keep=0):
+        while len(started) > keep:
+            started.pop(0).wait_send()
 
     def arrive(dst, ssem, rsem):
         remote(dst, dst, ssem, rsem, other).wait_recv()
@@ -87,6 +95,7 @@
     peers = [(ri, (bas + i) % NBAS) for i in range(1, NBAS)]
     peers += [z_peer(i) for i in range(1, NZ)]
     peers += [xy_peer(i) for i in range(1, NX * NYL)]
+    peers += [(at(x, 1 - yl, z), ((yh + i) % NYH) * NC + core) for i in (1, 3)]
     for dev in peers:
         pl.semaphore_signal(barrier, inc=1, device_id=dev, device_id_type=MESH)
 
@@ -147,12 +156,18 @@
         tile = jnp.concatenate([r[j * 4 : j * 4 + 4, :] for r in rows], axis=0)
         panel[j, ri, core] = tile.astype(BF16)
 
-    mine = panel.at[:, ri, core]
-    for i in range(1, NZ):
-        send(mine, mine, s_z.at[i], r_z.at[i], z_peer(i))
-    for i in range(1, NZ):
-        src = at(x, yl, (z - i + NZ) % NZ)
-        arrive(panel.at[:, src, core], s_z.at[i], r_z.at[i])
+    parts = (pl.ds(0, 1), pl.ds(1, NJ - 1))
+    for k, part_ in enumerate(parts):
+        mine = panel.at[part_, ri, core]
+        for i in range(1, NZ):
+            send(mine, mine, s_z.at[k, i], r_z.at[k, i], z_peer(i))
+
+    def arrive_z(k):
+        for i in range(1, NZ):
+            src = at(x, yl, (z - i + NZ) % NZ)
+            arrive(panel.at[parts[k], src, core], s_z.at[k, i], r_z.at[k, i])
+
+    arrive_z(0)
 
     def line_of(j, line_):
         return panel.at[j, pl.ds(line_ * NZ, NZ), core]
@@ -166,6 +181,7 @@
     for i in range(1, NX * NYL):
         send(mine, mine, s_xy.at[i], r_xy.at[i], xy_peer(i))
     pass_core(line)
+    arrive_z(1)
     for j in range(1, NJ):
         mine = line_of(j, line)
         send(mine, mine, s_pair.at[j], r_pair.at[j], pair)
@@ -181,8 +197,17 @@
         for i in range(1, NX):
             send(mine, mine, s_line.at[j, 1, i], r_line.at[j, 1, i], x_peer(i))
 
-    left, right = (yh - 1 + NYH) % NYH, (yh + 1) % NYH
+    before, after = (yh - 1 + NYH) % NYH, (yh + 1) % NYH
     across = (yh + 2) % NYH
+
+    def pass_near(j):
+        for s in range(2):
+            mine = near.at[s, core, j]
+            arrive(mine, s_y.at[j, s], r_y.at[j, s])
+            d = 1 - 2 * s
+            p = ((y + d + NYL * NYH) % (NYL * NYH)) // 4
+            send(near.at[s, core, j, p], far.at[s, core, j], s_y.at[j, 2 + s], r_y.at[j, 2 + s], y_chip(d))
+            send(mine, mine, s_hc.at[j, 1 + s], r_hc.at[j, 1 + s], other)
 
     for j in range(NJ):
         if j == 0:
@@ -208,33 +233,30 @@
         columns = panel[j].reshape(NBLK * BLK, LW)
         rows = jnp.dot(dense[...], columns, preferred_element_type=F32).astype(BF16)
         for p in range(RB):
-            half[bas, j, :, p * LW : (p + 1) * LW] = rows[p * ROWS : (p + 1) * ROWS, :]
-        mine = half.at[bas, j]
-        send(mine, mine, s_y.at[j, 0], r_y.at[j, 0], y_peer(1))
-        send(mine, mine, s_y.at[j, 1], r_y.at[j, 1], y_peer(3))
+            half[core, j, p] = rows[p * ROWS : (p + 1) * ROWS, :]
+        mine = half.at[core, j]
+        send(mine, near.at[0, core, j], s_y.at[j, 0], r_y.at[j, 0], y_chip(1))
+        send(mine, near.at[1, core, j], s_y.at[j, 1], r_y.at[j, 1], y_chip(-1))
         send(mine, mine, s_hc.at[j, 0], r_hc.at[j, 0], other)
         if j + 2 < NJ:
             pass_own(j + 2)
             pass_pair(j + 2)
-
-    def block(yh_):
-        return half.at[yh_ * NC + core]
-
-    def far_block(yh_):
-        return half.at[yh_ * NC + 1 - core]
-
-    def multiply(g, yh_, c, chunks, first=True, last=True):
-        cols = pl.ds(pl.multiple_of(c * ROWS, ROWS), ROWS)
-        total = jnp.zeros((ROWS, ROWS), F32) if first else part[g, :, cols]
-        for j in chunks:
-            total += lax.dot_general(
-                half[bas, j], half[yh_ * NC + c, j], (((1,), (1,)), ((), ())), preferred_element_type=F32
-            )
-        part[g, :, cols] = total
-        if last:
-            sent[g, :, cols] = total.astype(BF16)
-
-    def send_x(g):
+        if j >= 2:
+            pass_near(j - 2)
+
+    same, away = 1 - yl, yl
+    away_yh = jnp.where(yl == 1, after, before)
+
+    def wide(ref, *at_):
+        return jnp.concatenate([ref[(*at_, p)] for p in range(RB)], axis=1)
+
+    def multiply(g, rows, columns):
+        for c in range(NC):
+            total = jnp.zeros((ROWS, ROWS), F32)
+            for lhs, rhs in zip(rows, columns(c), strict=True):
+                total += lax.dot_general(lhs, rhs, (((1,), (1,)), ((), ())), preferred_element_type=F32)
+            part[g, :, c * ROWS : (c + 1) * ROWS] = total
+            sent[g, :, c * ROWS : (c + 1) * ROWS] = total.astype(BF16)
         for i in range(1, NX):
             x_ = (x + i) % NX
             send(sent.at[g, pl.ds(x_ * XR, XR)], got.at[g, i], s_x.at[g, i], r_x.at[g, i], x_peer(i))
@@ -253,6 +275,10 @@
         for i in range(1, NZ):
             send(share.at[g, (z + i) % NZ], land.at[g, z], s_f.at[g, i], r_f.at[g, i], z_peer(i))
 
+    def give(g, yl_, yh_, slot, k):
+        dev = (at(x, yl_, z), yh_ * NC + core)
+        send(last.at[g, yl_], fin.at[slot], s_fin.at[k], r_fin.at[slot], dev)
+
     def fold_z(g):
         for i in range(1, NZ):
             arrive(land.at[g, (z - i + NZ) % NZ], s_f.at[g, i], r_f.at[g, i])
@@ -261,108 +287,70 @@
             for z_ in range(1, NZ):
                 total += land[g, z_, yl_]
             last[g, yl_] = total
-        send(last.at[g, 1 - yl], last_got.at[g], s_f.at[g, 0], r_f.at[g, 0], pair)
-
-    def finish(g, yh_):
-        arrive(last_got.at[g], s_f.at[g, 0], r_f.at[g, 0])
-        out_ref[:, pl.ds(pl.multiple_of(yh_ * GW, GW), GW)] = -0.25 * (last[g, yl] + last_got[g])
-
-    for j in range(NJ):
-        arrive(far_block(yh).at[j], s_hc.at[j, 0], r_hc.at[j, 0])
-    for c in range(NC):
-        multiply(0, yh, c, range(NJ))
-    send_x(0)
-
-    def forward(j):
-        if j % 2 == 0:
-            mine = block(left).at[j]
-            send(mine, mine, s_y.at[j, 2], r_y.at[j, 2], y_peer(1))
+        if g < 2:
+            give(g, 1 - yl, yh, g, g)
         else:
-            mine = block(right).at[j]
-            send(mine, mine, s_y.at[j, 2], r_y.at[j, 2], y_peer(3))
-
-    for j in range(NJ):
-        mine = block(left).at[j]
-        arrive(mine, s_y.at[j, 0], r_y.at[j, 0])
-        send(mine, mine, s_hc.at[j, 1], r_hc.at[j, 1], other)
-        mine = block(right).at[j]
-        arrive(mine, s_y.at[j, 1], r_y.at[j, 1])
-        send(mine, mine, s_hc.at[j, 2], r_hc.at[j, 2], other)
-        if j == 0:
-            fold_x(0)
-        if j == NJ - 2:
-            forward(0)
-            forward(1)
-    for j in range(2, NJ):
-        forward(j)
-    for g, yh_ in ((1, left), (2, right)):
-        for j in range(NJ):
-            arrive(far_block(yh_).at[j], s_hc.at[j, g], r_hc.at[j, g])
-        for c in range(NC):
-            multiply(g, yh_, c, range(NJ))
-        send_x(g)
-    def far(chunks):
-        for j in chunks:
-            mine = block(across).at[j]
-            arrive(mine, s_y.at[j, 2], r_y.at[j, 2])
-            send(mine, mine, s_hc.at[j, 3], r_hc.at[j, 3], other)
-
-    def far_other(chunks):
-        for j in chunks:
-            arrive(far_block(across).at[j], s_hc.at[j, 3], r_hc.at[j, 3])
-
-    def last_parts(i, c):
-        cols = pl.ds(pl.multiple_of(c * ROWS, ROWS), ROWS)
-        return got.at[3, i // NYL, pl.ds((i % NYL) * 32, 32), cols], cols
-
-    def send_last(k, c):
-        for i in range(1, NX * NYL):
-            line_ = ((x + i // NYL) % NX) * NYL + (yl + i % NYL) % NYL
-            dst, cols = last_parts(i, c)
-            send(sent.at[3, pl.ds(line_ * 32, 32), cols], dst, s_last.at[k, i], r_last.at[k, i], xy_peer(i))
-
-    far((0, 1))
-    fold_x(1)
-    far_other((0, 1))
-    for c in range(NC):
-        multiply(3, across, c, (0, 1), True, False)
-    fold_x(2)
-    far((2, 3))
-    multiply(3, across, core, (2, 3), False, True)
-    send_last(0, core)
-    far_other((2, 3))
-    multiply(3, across, 1 - core, (2, 3), False, True)
-    send_last(1, 1 - core)
-    for g in range(3):
-        fold_z(g)
-    for k, c in ((0, core), (1, 1 - core)):
-        for i in range(1, NX * NYL):
-            arrive(last_parts(i, c)[0], s_last.at[k, i], r_last.at[k, i])
-    total = part[3, pl.ds(line * 32, 32), :]
-    for i in range(1, NX * NYL):
-        total += got[3, i // NYL, (i % NYL) * 32 : (i % NYL) * 32 + 32, :].astype(F32)
-    for i in range(NZ):
-        share[3, i, 0] = total[i * 4 : i * 4 + 4, :]
-    land[3, z, 0] = share[3, z, 0]
-    for i in range(1, NZ):
-        src, dst = share.at[3, (z + i) % NZ, 0], land.at[3, z, 0]
-        send(src, dst, s_f.at[3, i], r_f.at[3, i], z_peer(i))
-    finish(0, yh)
-    finish(1, left)
-    finish(2, right)
-    for i in range(1, NZ):
-        arrive(land.at[3, (z - i + NZ) % NZ, 0], s_f.at[3, i], r_f.at[3, i])
-    total = land[3, 0, 0]
-    for i in range(1, NZ):
-        total += land[3, i, 0]
-    out_ref[:, pl.ds(pl.multiple_of(across * GW, GW), GW)] = -0.25 * total
-
-    for copy in started:
-        copy.wait_send()
+            for yl_ in range(NYL):
+                yh_ = (away_yh, before, after)[g - 2]
+                give(g, yl_, yh_, g * 2 - 2 + yl, g * 2 - 2 + yl_)
+
+    drain(9)
 
     @pl.when(jnp.logical_not(own_head))
     def _():
         head_copy(0).wait_send()
+
+    for j in range(NJ):
+        arrive(half.at[1 - core, j], s_hc.at[j, 0], r_hc.at[j, 0])
+    multiply(0, [wide(half, core, j) for j in range(NJ)], lambda c: [wide(half, c, j) for j in range(NJ)])
+    for j in (NJ - 2, NJ - 1):
+        pass_near(j)
+    for j in range(NJ):
+        for s in range(2):
+            arrive(near.at[s, 1 - core, j], s_hc.at[j, 1 + s], r_hc.at[j, 1 + s])
+    for g, r, o in ((1, same, away), (2, away, same)):
+        multiply(g, [wide(near, r, core, j) for j in range(NJ)], lambda c, o=o: [wide(near, o, c, j) for j in range(NJ)])
+    fold_x(0)
+    for j in range(NJ):
+        for s in range(2):
+            mine = far.at[s, core, j]
+            arrive(mine, s_y.at[j, 2 + s], r_y.at[j, 2 + s])
+            send(mine, mine, s_hc.at[j, 3 + s], r_hc.at[j, 3 + s], other)
+    for j in range(NJ):
+        for s in range(2):
+            arrive(far.at[s, 1 - core, j], s_hc.at[j, 3 + s], r_hc.at[j, 3 + s])
+
+    def pairs(s, c):
+        return [jnp.concatenate([far[s, c, j], far[s, c, j + 1]], axis=1) for j in range(0, NJ, 2)]
+
+    for g, s in ((3, 0), (4, 1)):
+        multiply(g, pairs(s, core), lambda c, s=s: pairs(1 - s, c))
+    fold_x(1)
+    fold_x(2)
+    fold_z(0)
+    fold_x(3)
+    fold_z(1)
+    fold_x(4)
+    fold_z(2)
+    drain(21)
+    fold_z(3)
+    fold_z(4)
+
+    def put(yh_, value):
+        out_ref[:, pl.ds(pl.multiple_of(yh_ * GW, GW), GW)] = -0.25 * value
+
+    def came(slot):
+        arrive(fin.at[slot], s_fin.at[slot], r_fin.at[slot])
+
+    for slot in range(4):
+        came(slot)
+    put(yh, last[0, yl] + fin[0])
+    put(away_yh, last[1, yl] + fin[3 - yl])
+    put(jnp.where(yl == 1, before, after), fin[1] + fin[2 + yl])
+    for slot in range(4, 8):
+        came(slot)
+    put(across, (fin[4] + fin[5]) + (fin[6] + fin[7]))
+    drain()
 
 
 def local(three_centre, slot_index, slot_count, panel_last, panel_prev, panel_older):
@@ -385,27 +373,29 @@
             pltpu.VMEM((16, BLK), BF16),
             pltpu.VMEM((4, 16, BLK), BF16),
             pltpu.VMEM((NJ, NRI, 2, 16, LW), BF16),
-            pltpu.VMEM((NBAS, NJ, ROWS, RB * LW), BF16),
-            pltpu.VMEM((4, ROWS, GW), F32),
-            pltpu.VMEM((4, ROWS, GW), BF16),
-            pltpu.VMEM((4, NX, XR, GW), BF16),
-            pltpu.VMEM((4, NZ, NYL, 4, GW), F32),
-            pltpu.VMEM((4, NZ, NYL, 4, GW), F32),
-            pltpu.VMEM((3, NYL, 4, GW), F32),
-            pltpu.VMEM((3, 4, GW), F32),
+            pltpu.VMEM((NC, NJ, RB, ROWS, LW), BF16),
+            pltpu.VMEM((2, NC, NJ, RB, ROWS, LW), BF16),
+            pltpu.VMEM((2, NC, NJ, ROWS, LW), BF16),
+            pltpu.VMEM((5, ROWS, GW), F32),
+            pltpu.VMEM((5, ROWS, GW), BF16),
+            pltpu.VMEM((5, NX, XR, GW), BF16),
+            pltpu.VMEM((5, NZ, NYL, 4, GW), F32),
+            pltpu.VMEM((5, NZ, NYL, 4, GW), F32),
+            pltpu.VMEM((5, NYL, 4, GW), F32),
+            pltpu.VMEM((8, 4, GW), F32),
             dma((7,)),
             dma((NYH,)), dma((4,)),
-            dma((NZ,)), dma((NZ,)),
+            dma((2, NZ)), dma((2, NZ)),
             dma((NX * NYL,)), dma((NX * NYL,)),
             dma((NX * NYL,)), dma((NX * NYL,)),
             dma((NJ,)), dma((NJ,)),
             dma((NJ, NYL, NX)), dma((NJ, NYL, NX)),
             dma((NJ,)), dma((NJ,)),
-            dma((NJ, 3)), dma((NJ, 3)),
             dma((NJ, 4)), dma((NJ, 4)),
-            dma((3, NX)), dma((3, NX)),
-            dma((4, NZ)), dma((4, NZ)),
-            dma((NC, NX * NYL)), dma((NC, NX * NYL)),
+            dma((NJ, 5)), dma((NJ, 5)),
+            dma((5, NX)), dma((5, NX)),
+            dma((5, NZ)), dma((5, NZ)),
+            dma((8,)), dma((8,)),
         ],
         compiler_params=pltpu.CompilerParams(
             collective_id=0, has_side_effects=True, vmem_limit_bytes=60 * 1024 * 1024

time: 88 us -> 79.7 us (0.906)
  Pallas kernels: 85.7 us -> 77.5 us
    pallas_call x1, Pallas kernels: 85.7 us -> 77.5 us  [local(): pl.pallas_call(kernel, out_shape=jax.ShapeDtypeStruct((4, NBLK * BLK), F3...]
where the time goes in v4:
time: 79.7 us; the launch traced here: 79.5 us
  Pallas kernels  77.5 us (97%)
  local copies, waits for them, and re-layouts  1.38 us (2%)
    pallas_call x1, Pallas kernels, local(): pl.pallas_call(kernel, out_shape=jax.ShapeDtypeStruct((4, NBLK * BLK), F3...  77.5 us

profile of v4, /device:TPU:1, one launch (start us, length us, event | category | flops | bytes accessed | tf_op | source)
XLA Modules:
  0.0 79.5 jit_solution(6628727117726479574)
XLA Ops:
  0.7 77.5 %shard_map.64 = f32[4,2048]{1,0:T(4,128)} custom-call(bf16[32,2,128,128]{3,2,1,0:T(8,128)(2,1)} %bitcast.4, s32[1,3,1,32]{3,2,1,0:T(1,128)} %bitcast.5, s32[1,1]{1,0:T(1,128)S(6)} %copy.8.count_hbm, bf16[4,512]{1,0:T(4,128)(2,1)} %last_hbm.1, bf16[4,512]{1,0:T(4,128)(2,1)} %prev_hbm.1, bf16[4,512]{1,0:T(4,128)(2,1)} %older_hbm.1), custom_call_target="tpu_custom_call" | custom-call | flops 2147483648 | bytes 3145728 | tf_op jit(solution)/shard_map/pallas_call | solution.py:360
  78.1 1.4 %copy.9 = f32[1,1,4,2048]{3,2,1,0:T(4,128)} copy(f32[1,1,4,2048]{3,2,1,0:T(4,128)} %bitcast.3) | data formatting | bytes 65536

commit v5 on v4

--- a/solution.py
+++ b/solution.py
@@ -26,7 +26,7 @@
 def kernel(
     t_hbm, slots_hbm, count_hbm, last_hbm, prev_hbm, older_hbm, out_ref,
     t_v, slots_v, count_v, panels_v, table_v, table, dense, pred, heads, panel, half, near, far,
-    part, sent, got, share, land, last, fin,
+    part, sent, got, share, land, share_b, land_b, last, fin,
     in_sem,
     s_head, r_head, s_z, r_z, s_xy, r_xy, s_lc, r_lc, s_pair, r_pair, s_line, r_line, s_core, r_core,
     s_y, r_y, s_hc, r_hc, s_x, r_x, s_f, r_f, s_fin, r_fin,
@@ -87,7 +87,7 @@
             (slots_hbm, slots_v), (count_hbm, count_v), (t_hbm, t_v),
         ))
     ]
-    for copy in loads:
+    for copy in loads[:3]:
         copy.start()
 
     barrier = pltpu.get_barrier_semaphore()
@@ -95,7 +95,6 @@
     peers = [(ri, (bas + i) % NBAS) for i in range(1, NBAS)]
     peers += [z_peer(i) for i in range(1, NZ)]
     peers += [xy_peer(i) for i in range(1, NX * NYL)]
-    peers += [(at(x, 1 - yl, z), ((yh + i) % NYH) * NC + core) for i in (1, 3)]
     for dev in peers:
         pl.semaphore_signal(barrier, inc=1, device_id=dev, device_id_type=MESH)
 
@@ -124,6 +123,9 @@
     @pl.when(jnp.logical_not(own_head))
     def _():
         head_copy(0).start()
+
+    for copy in loads[3:]:
+        copy.start()
 
     loads[3].wait()
     loads[4].wait()
@@ -159,7 +161,7 @@
     parts = (pl.ds(0, 1), pl.ds(1, NJ - 1))
     for k, part_ in enumerate(parts):
         mine = panel.at[part_, ri, core]
-        for i in range(1, NZ):
+        for i in (4, 3, 5, 2, 6, 1, 7):
             send(mine, mine, s_z.at[k, i], r_z.at[k, i], z_peer(i))
 
     def arrive_z(k):
@@ -178,7 +180,7 @@
         send(mine, mine, s_lc.at[line_], r_lc.at[line_], other)
 
     mine = line_of(0, line)
-    for i in range(1, NX * NYL):
+    for i in (5, 4, 3, 7, 2, 6, 1):
         send(mine, mine, s_xy.at[i], r_xy.at[i], xy_peer(i))
     pass_core(line)
     arrive_z(1)
@@ -204,10 +206,13 @@
         for s in range(2):
             mine = near.at[s, core, j]
             arrive(mine, s_y.at[j, s], r_y.at[j, s])
+            send(mine, mine, s_hc.at[j, 1 + s], r_hc.at[j, 1 + s], other)
+
+    def pass_far(j):
+        for s in range(2):
             d = 1 - 2 * s
             p = ((y + d + NYL * NYH) % (NYL * NYH)) // 4
             send(near.at[s, core, j, p], far.at[s, core, j], s_y.at[j, 2 + s], r_y.at[j, 2 + s], y_chip(d))
-            send(mine, mine, s_hc.at[j, 1 + s], r_hc.at[j, 1 + s], other)
 
     for j in range(NJ):
         if j == 0:
@@ -223,6 +228,9 @@
                 x_ = (x - i + NX) % NX
                 arrive(line_of(j, x_ * NYL + yl), s_line.at[j, 0, i], r_line.at[j, 0, i])
                 arrive(line_of(j, x_ * NYL + 1 - yl), s_line.at[j, 1, i], r_line.at[j, 1, i])
+        if j + 2 < NJ:
+            pass_own(j + 2)
+            pass_pair(j + 2)
         if j == 0:
             for line_ in range(NX * NYL):
                 arrive(panel.at[0, pl.ds(line_ * NZ, NZ), 1 - core], s_lc.at[line_], r_lc.at[line_])
@@ -238,9 +246,6 @@
         send(mine, near.at[0, core, j], s_y.at[j, 0], r_y.at[j, 0], y_chip(1))
         send(mine, near.at[1, core, j], s_y.at[j, 1], r_y.at[j, 1], y_chip(-1))
         send(mine, mine, s_hc.at[j, 0], r_hc.at[j, 0], other)
-        if j + 2 < NJ:
-            pass_own(j + 2)
-            pass_pair(j + 2)
         if j >= 2:
             pass_near(j - 2)
 
@@ -268,25 +273,36 @@
         for i in range(1, NX):
             total += got[g, i].astype(F32)
         for z_ in range(NZ):
-            for yl_ in range(NYL):
-                k = (yl_ * NZ + z_) * 4
-                share[g, z_, yl_] = total[k : k + 4, :]
-        land[g, z] = share[g, z]
-        for i in range(1, NZ):
-            send(share.at[g, (z + i) % NZ], land.at[g, z], s_f.at[g, i], r_f.at[g, i], z_peer(i))
+            pieces = [total[(yl_ * NZ + z_) * 4 : (yl_ * NZ + z_) * 4 + 4, :] for yl_ in range(NYL)]
+            if g == 0:
+                for yl_ in range(NYL):
+                    share[z_, yl_] = pieces[yl_]
+            else:
+                tile = jnp.concatenate([p[:, h * 256 : h * 256 + 256] for h in range(2) for p in pieces], axis=0)
+                share_b[g - 1, z_] = tile.astype(BF16)
+        src, dst = (share, land) if g == 0 else (share_b.at[g - 1], land_b.at[g - 1])
+        dst[z] = src[z]
+        for i in (4, 3, 5, 2, 6, 1, 7):
+            send(src.at[(z + i) % NZ], dst.at[z], s_f.at[g, i], r_f.at[g, i], z_peer(i))
 
     def give(g, yl_, yh_, slot, k):
         dev = (at(x, yl_, z), yh_ * NC + core)
         send(last.at[g, yl_], fin.at[slot], s_fin.at[k], r_fin.at[slot], dev)
 
     def fold_z(g):
+        dst = land if g == 0 else land_b.at[g - 1]
         for i in range(1, NZ):
-            arrive(land.at[g, (z - i + NZ) % NZ], s_f.at[g, i], r_f.at[g, i])
+            arrive(dst.at[(z - i + NZ) % NZ], s_f.at[g, i], r_f.at[g, i])
+        total = dst[0].astype(F32)
+        for z_ in range(1, NZ):
+            total += dst[z_].astype(F32)
         for yl_ in range(NYL):
-            total = land[g, 0, yl_]
-            for z_ in range(1, NZ):
-                total += land[g, z_, yl_]
-            last[g, yl_] = total
+            if g == 0:
+                last[g, yl_] = total[yl_]
+            else:
+                for h in range(2):
+                    k = (h * NYL + yl_) * 4
+                    last[g, yl_, :, h * 256 : h * 256 + 256] = total[k : k + 4, :]
         if g < 2:
             give(g, 1 - yl, yh, g, g)
         else:
@@ -303,8 +319,11 @@
     for j in range(NJ):
         arrive(half.at[1 - core, j], s_hc.at[j, 0], r_hc.at[j, 0])
     multiply(0, [wide(half, core, j) for j in range(NJ)], lambda c: [wide(half, c, j) for j in range(NJ)])
-    for j in (NJ - 2, NJ - 1):
-        pass_near(j)
+    pass_near(NJ - 2)
+    for j in range(NJ - 1):
+        pass_far(j)
+    pass_near(NJ - 1)
+    pass_far(NJ - 1)
     for j in range(NJ):
         for s in range(2):
             arrive(near.at[s, 1 - core, j], s_hc.at[j, 1 + s], r_hc.at[j, 1 + s])
@@ -379,8 +398,10 @@
             pltpu.VMEM((5, ROWS, GW), F32),
             pltpu.VMEM((5, ROWS, GW), BF16),
             pltpu.VMEM((5, NX, XR, GW), BF16),
-            pltpu.VMEM((5, NZ, NYL, 4, GW), F32),
-            pltpu.VMEM((5, NZ, NYL, 4, GW), F32),
+            pltpu.VMEM((NZ, NYL, 4, GW), F32),
+            pltpu.VMEM((NZ, NYL, 4, GW), F32),
+            pltpu.VMEM((4, NZ, 16, 256), BF16),
+            pltpu.VMEM((4, NZ, 16, 256), BF16),
             pltpu.VMEM((5, NYL, 4, GW), F32),
             pltpu.VMEM((8, 4, GW), F32),
             dma((7,)),

time: 79.7 us -> 76.3 us (0.957)
  Pallas kernels: 77.5 us -> 73.8 us
    pallas_call x1, Pallas kernels: 77.5 us -> 73.8 us  [local(): pl.pallas_call(kernel, out_shape=jax.ShapeDtypeStruct((4, NBLK * BLK), F3...]
where the time goes in v5:
time: 76.3 us; the launch traced here: 75.8 us
  Pallas kernels  73.8 us (97%)
  local copies, waits for them, and re-layouts  1.38 us (2%)
    pallas_call x1, Pallas kernels, local(): pl.pallas_call(kernel, out_shape=jax.ShapeDtypeStruct((4, NBLK * BLK), F3...  73.8 us

profile of v5, /device:TPU:1, one launch (start us, length us, event | category | flops | bytes accessed | tf_op | source)
XLA Modules:
  0.0 75.8 jit_solution(12188635461802474055)
XLA Ops:
  0.7 73.8 %shard_map.64 = f32[4,2048]{1,0:T(4,128)} custom-call(bf16[32,2,128,128]{3,2,1,0:T(8,128)(2,1)} %bitcast.4, s32[1,3,1,32]{3,2,1,0:T(1,128)} %bitcast.5, s32[1,1]{1,0:T(1,128)S(6)} %copy.8.count_hbm, bf16[4,512]{1,0:T(4,128)(2,1)} %last_hbm.1, bf16[4,512]{1,0:T(4,128)(2,1)} %prev_hbm.1, bf16[4,512]{1,0:T(4,128)(2,1)} %older_hbm.1), custom_call_target="tpu_custom_call" | custom-call | flops 2147483648 | bytes 3145728 | tf_op jit(solution)/shard_map/pallas_call | solution.py:379
  74.4 1.4 %copy.9 = f32[1,1,4,2048]{3,2,1,0:T(4,128)} copy(f32[1,1,4,2048]{3,2,1,0:T(4,128)} %bitcast.3) | data formatting | bytes 65536

commit v6 on v5

--- a/solution.py
+++ b/solution.py
@@ -26,14 +26,19 @@
 def kernel(
     t_hbm, slots_hbm, count_hbm, last_hbm, prev_hbm, older_hbm, out_ref,
     t_v, slots_v, count_v, panels_v, table_v, table, dense, pred, heads, panel, half, near, far,
-    part, sent, got, share, land, share_b, land_b, last, fin,
+    part, sent, got, share, land, share_b, land_b, share_c, land_c, last, fin,
     in_sem,
     s_head, r_head, s_z, r_z, s_xy, r_xy, s_lc, r_lc, s_pair, r_pair, s_line, r_line, s_core, r_core,
-    s_y, r_y, s_hc, r_hc, s_x, r_x, s_f, r_f, s_fin, r_fin,
+    s_y, r_y, s_hc, r_hc, s_x, r_x, s_f, r_f, s_fin, r_fin, s_c, r_c,
 ):
     ri, bas = lax.axis_index("ri"), lax.axis_index("bas")
     x, yl, z = ri // (NYL * NZ), (ri // NZ) % NYL, ri % NZ
     yh, core = bas // NC, bas % NC
+
+    def ring(v, n):
+        return [v] + [jnp.where(v + i >= n, v + i - n, v + i) for i in range(1, n)]
+
+    xs, yls, zs, yhs = ring(x, NX), [yl, 1 - yl], ring(z, NZ), ring(yh, NYH)
     line = x * NYL + yl
     other = (ri, yh * NC + 1 - core)
     head_core = bas // 4
@@ -43,22 +48,20 @@
         return (x_ * NYL + yl_) * NZ + z_
 
     def head_target(i):
-        return (ri, ((yh + i) % NYH) * NC + head_core)
+        return (ri, yhs[i % NYH] * NC + head_core)
 
     def z_peer(i):
-        return (at(x, yl, (z + i) % NZ), bas)
+        return (at(x, yl, zs[i]), bas)
 
     def x_peer(i):
-        return (at((x + i) % NX, yl, z), bas)
+        return (at(xs[i], yl, z), bas)
 
     def xy_peer(i):
-        return (at((x + i // NYL) % NX, (yl + i % NYL) % NYL, z), bas)
-
-    y = yh * NYL + yl
-
-    def y_chip(d):
-        y_ = (y + d + NYL * NYH) % (NYL * NYH)
-        return (at(x, y_ % NYL, z), (y_ // NYL) * NC + core)
+        return (at(xs[i // NYL], yls[i % NYL], z), bas)
+
+    next_yh, prev_yh = jnp.where(yl == 1, yhs[1], yh), jnp.where(yl == 1, yh, yhs[3])
+    next_chip = (at(x, 1 - yl, z), next_yh * NC + core)
+    prev_chip = (at(x, 1 - yl, z), prev_yh * NC + core)
 
     pair = (at(x, 1 - yl, z), bas)
     started = []
@@ -92,11 +95,23 @@
 
     barrier = pltpu.get_barrier_semaphore()
 
-    peers = [(ri, (bas + i) % NBAS) for i in range(1, NBAS)]
-    peers += [z_peer(i) for i in range(1, NZ)]
+    def greet(dev):
+        pl.semaphore_signal(barrier, inc=1, device_id=dev, device_id_type=MESH)
+
+    own_head = core == head_core
+    for k in range(4):
+        @pl.when(4 * core + k != bas)
+        def _():
+            greet((ri, 4 * core + k))
+
+    @pl.when(jnp.logical_not(own_head))
+    def _():
+        greet(other)
+
+    peers = [z_peer(i) for i in range(1, NZ)]
     peers += [xy_peer(i) for i in range(1, NX * NYL)]
     for dev in peers:
-        pl.semaphore_signal(barrier, inc=1, device_id=dev, device_id_type=MESH)
+        greet(dev)
 
     for copy in loads[:3]:
         copy.wait()
@@ -104,13 +119,11 @@
     mixed = 2.5 * panels[0] - 2.0 * panels[1] + 0.5 * panels[2]
     packed = jnp.concatenate([mixed[:, j * LW : (j + 1) * LW] for j in range(NJ)], axis=0).astype(BF16)
     pred[...] = packed
-    own_head = core == head_core
-
     @pl.when(own_head)
     def _():
         heads[head_slot] = packed
 
-    pl.semaphore_wait(barrier, len(peers))
+    pl.semaphore_wait(barrier, 4 + len(peers))
 
     def head_copy(i):
         return remote(pred, heads.at[head_slot], s_head.at[i], r_head.at[head_slot], head_target(i))
@@ -166,7 +179,7 @@
 
     def arrive_z(k):
         for i in range(1, NZ):
-            src = at(x, yl, (z - i + NZ) % NZ)
+            src = at(x, yl, zs[NZ - i])
             arrive(panel.at[parts[k], src, core], s_z.at[k, i], r_z.at[k, i])
 
     arrive_z(0)
@@ -190,17 +203,16 @@
 
     def pass_own(j):
         mine = line_of(j, line)
-        for i in range(1, NX):
+        for i in (2, 1, 3):
             send(mine, mine, s_line.at[j, 0, i], r_line.at[j, 0, i], x_peer(i))
 
     def pass_pair(j):
         mine = line_of(j, pair_line)
         arrive(mine, s_pair.at[j], r_pair.at[j])
-        for i in range(1, NX):
+        for i in (2, 1, 3):
             send(mine, mine, s_line.at[j, 1, i], r_line.at[j, 1, i], x_peer(i))
 
-    before, after = (yh - 1 + NYH) % NYH, (yh + 1) % NYH
-    across = (yh + 2) % NYH
+    before, after, across = yhs[3], yhs[1], yhs[2]
 
     def pass_near(j):
         for s in range(2):
@@ -210,14 +222,13 @@
 
     def pass_far(j):
         for s in range(2):
-            d = 1 - 2 * s
-            p = ((y + d + NYL * NYH) % (NYL * NYH)) // 4
-            send(near.at[s, core, j, p], far.at[s, core, j], s_y.at[j, 2 + s], r_y.at[j, 2 + s], y_chip(d))
+            dev, p = ((next_chip, next_yh // 2), (prev_chip, prev_yh // 2))[s]
+            send(near.at[s, core, j, p], far.at[s, core, j], s_y.at[j, 2 + s], r_y.at[j, 2 + s], dev)
 
     for j in range(NJ):
         if j == 0:
             for i in (1, 2, 6, 3, 7, 4, 5):
-                line_ = ((x - i // NYL + NX) % NX) * NYL + (yl + i % NYL) % NYL
+                line_ = xs[(NX - i // NYL) % NX] * NYL + yls[i % NYL]
                 arrive(line_of(0, line_), s_xy.at[i], r_xy.at[i])
                 pass_core(line_)
                 if i == 6:
@@ -225,7 +236,7 @@
             pass_pair(1)
         else:
             for i in range(1, NX):
-                x_ = (x - i + NX) % NX
+                x_ = xs[NX - i]
                 arrive(line_of(j, x_ * NYL + yl), s_line.at[j, 0, i], r_line.at[j, 0, i])
                 arrive(line_of(j, x_ * NYL + 1 - yl), s_line.at[j, 1, i], r_line.at[j, 1, i])
         if j + 2 < NJ:
@@ -243,8 +254,8 @@
         for p in range(RB):
             half[core, j, p] = rows[p * ROWS : (p + 1) * ROWS, :]
         mine = half.at[core, j]
-        send(mine, near.at[0, core, j], s_y.at[j, 0], r_y.at[j, 0], y_chip(1))
-        send(mine, near.at[1, core, j], s_y.at[j, 1], r_y.at[j, 1], y_chip(-1))
+        send(mine, near.at[0, core, j], s_y.at[j, 0], r_y.at[j, 0], next_chip)
+        send(mine, near.at[1, core, j], s_y.at[j, 1], r_y.at[j, 1], prev_chip)
         send(mine, mine, s_hc.at[j, 0], r_hc.at[j, 0], other)
         if j >= 2:
             pass_near(j - 2)
@@ -262,8 +273,8 @@
                 total += lax.dot_general(lhs, rhs, (((1,), (1,)), ((), ())), preferred_element_type=F32)
             part[g, :, c * ROWS : (c + 1) * ROWS] = total
             sent[g, :, c * ROWS : (c + 1) * ROWS] = total.astype(BF16)
-        for i in range(1, NX):
-            x_ = (x + i) % NX
+        for i in (2, 1, 3):
+            x_ = xs[i]
             send(sent.at[g, pl.ds(x_ * XR, XR)], got.at[g, i], s_x.at[g, i], r_x.at[g, i], x_peer(i))
 
     def fold_x(g):
@@ -272,6 +283,18 @@
         total = part[g, pl.ds(x * XR, XR), :]
         for i in range(1, NX):
             total += got[g, i].astype(F32)
+        if g > 2:
+            for k in range(NYL * NZ):
+                piece = total[k * 4 : k * 4 + 4, :]
+                tile = jnp.concatenate([piece[:, h * BLK : h * BLK + BLK] for h in range(4)], axis=0)
+                share_c[g - 3, k // NZ, k % NZ] = tile.astype(BF16)
+            yh_ = (before, after)[g - 3]
+            for i in (4, 3, 5, 2, 6, 1, 7, 0):
+                for yl_ in range(NYL):
+                    z_ = zs[i]
+                    dev = (at(x, yl_, z_), yh_ * NC + core)
+                    send(share_c.at[g - 3, yl_, z_], land_c.at[g - 3, yl, z], s_c.at[g - 3, yl_, i], r_c.at[g - 3, yl, i], dev)
+            return
         for z_ in range(NZ):
             pieces = [total[(yl_ * NZ + z_) * 4 : (yl_ * NZ + z_) * 4 + 4, :] for yl_ in range(NYL)]
             if g == 0:
@@ -283,7 +306,7 @@
         src, dst = (share, land) if g == 0 else (share_b.at[g - 1], land_b.at[g - 1])
         dst[z] = src[z]
         for i in (4, 3, 5, 2, 6, 1, 7):
-            send(src.at[(z + i) % NZ], dst.at[z], s_f.at[g, i], r_f.at[g, i], z_peer(i))
+            send(src.at[zs[i]], dst.at[z], s_f.at[g, i], r_f.at[g, i], z_peer(i))
 
     def give(g, yl_, yh_, slot, k):
         dev = (at(x, yl_, z), yh_ * NC + core)
@@ -292,7 +315,7 @@
     def fold_z(g):
         dst = land if g == 0 else land_b.at[g - 1]
         for i in range(1, NZ):
-            arrive(dst.at[(z - i + NZ) % NZ], s_f.at[g, i], r_f.at[g, i])
+            arrive(dst.at[zs[(NZ - i) % NZ]], s_f.at[g, i], r_f.at[g, i])
         total = dst[0].astype(F32)
         for z_ in range(1, NZ):
             total += dst[z_].astype(F32)
@@ -307,8 +330,7 @@
             give(g, 1 - yl, yh, g, g)
         else:
             for yl_ in range(NYL):
-                yh_ = (away_yh, before, after)[g - 2]
-                give(g, yl_, yh_, g * 2 - 2 + yl, g * 2 - 2 + yl_)
+                give(g, yl_, away_yh, 2 + yl, 2 + yl_)
 
     drain(9)
 
@@ -348,12 +370,10 @@
     fold_x(2)
     fold_z(0)
     fold_x(3)
+    fold_x(4)
     fold_z(1)
-    fold_x(4)
     fold_z(2)
-    drain(21)
-    fold_z(3)
-    fold_z(4)
+    drain()
 
     def put(yh_, value):
         out_ref[:, pl.ds(pl.multiple_of(yh_ * GW, GW), GW)] = -0.25 * value
@@ -366,9 +386,15 @@
     put(yh, last[0, yl] + fin[0])
     put(away_yh, last[1, yl] + fin[3 - yl])
     put(jnp.where(yl == 1, before, after), fin[1] + fin[2 + yl])
-    for slot in range(4, 8):
-        came(slot)
-    put(across, (fin[4] + fin[5]) + (fin[6] + fin[7]))
+    total = jnp.zeros((16, BLK), F32)
+    for k in range(2):
+        for i in range(NZ):
+            for yl_ in range(NYL):
+                arrive(land_c.at[k, yl_, zs[(NZ - i) % NZ]], s_c.at[k, yl_, i], r_c.at[k, yl_, i])
+        for i in range(NZ):
+            for yl_ in range(NYL):
+                total += land_c[k, yl_, i].astype(F32)
+    put(across, jnp.concatenate([total[h * 4 : h * 4 + 4, :] for h in range(4)], axis=1))
     drain()
 
 
@@ -400,10 +426,12 @@
             pltpu.VMEM((5, NX, XR, GW), BF16),
             pltpu.VMEM((NZ, NYL, 4, GW), F32),
             pltpu.VMEM((NZ, NYL, 4, GW), F32),
-            pltpu.VMEM((4, NZ, 16, 256), BF16),
-            pltpu.VMEM((4, NZ, 16, 256), BF16),
-            pltpu.VMEM((5, NYL, 4, GW), F32),
-            pltpu.VMEM((8, 4, GW), F32),
+            pltpu.VMEM((2, NZ, 16, 256), BF16),
+            pltpu.VMEM((2, NZ, 16, 256), BF16),
+            pltpu.VMEM((2, NYL, NZ, 16, BLK), BF16),
+            pltpu.VMEM((2, NYL, NZ, 16, BLK), BF16),
+            pltpu.VMEM((3, NYL, 4, GW), F32),
+            pltpu.VMEM((4, 4, GW), F32),
             dma((7,)),
             dma((NYH,)), dma((4,)),
             dma((2, NZ)), dma((2, NZ)),
@@ -415,8 +443,9 @@
             dma((NJ, 4)), dma((NJ, 4)),
             dma((NJ, 5)), dma((NJ, 5)),
             dma((5, NX)), dma((5, NX)),
-            dma((5, NZ)), dma((5, NZ)),
-            dma((8,)), dma((8,)),
+            dma((3, NZ)), dma((3, NZ)),
+            dma((4,)), dma((4,)),
+            dma((2, NYL, NZ)), dma((2, NYL, NZ)),
         ],
         compiler_params=pltpu.CompilerParams(
             collective_id=0, has_side_effects=True, vmem_limit_bytes=60 * 1024 * 1024

time: 76.3 us -> 74.9 us (0.982)
  Pallas kernels: 73.8 us -> 72.6 us
    pallas_call x1, Pallas kernels: 73.8 us -> 72.6 us  [local(): pl.pallas_call(kernel, out_shape=jax.ShapeDtypeStruct((4, NBLK * BLK), F3...]
where the time goes in v6:
time: 74.9 us; the launch traced here: 74.6 us
  Pallas kernels  72.6 us (97%)
  local copies, waits for them, and re-layouts  1.38 us (2%)
    pallas_call x1, Pallas kernels, local(): pl.pallas_call(kernel, out_shape=jax.ShapeDtypeStruct((4, NBLK * BLK), F3...  72.6 us

profile of v6, /device:TPU:1, one launch (start us, length us, event | category | flops | bytes accessed | tf_op | source)
XLA Modules:
  0.0 74.6 jit_solution(2828959913318771299)
XLA Ops:
  0.7 72.6 %shard_map.64 = f32[4,2048]{1,0:T(4,128)} custom-call(bf16[32,2,128,128]{3,2,1,0:T(8,128)(2,1)} %bitcast.4, s32[1,3,1,32]{3,2,1,0:T(1,128)} %bitcast.5, s32[1,1]{1,0:T(1,128)S(6)} %copy.8.count_hbm, bf16[4,512]{1,0:T(4,128)(2,1)} %last_hbm.1, bf16[4,512]{1,0:T(4,128)(2,1)} %prev_hbm.1, bf16[4,512]{1,0:T(4,128)(2,1)} %older_hbm.1), custom_call_target="tpu_custom_call" | custom-call | flops 2147483648 | bytes 3145728 | tf_op jit(solution)/shard_map/pallas_call | solution.py:405
  73.3 1.4 %copy.9 = f32[1,1,4,2048]{3,2,1,0:T(4,128)} copy(f32[1,1,4,2048]{3,2,1,0:T(4,128)} %bitcast.3) | data formatting | bytes 65536

commit v7 on v6

--- a/solution.py
+++ b/solution.py
@@ -24,8 +24,8 @@
 
 
 def kernel(
-    t_hbm, slots_hbm, count_hbm, last_hbm, prev_hbm, older_hbm, out_ref,
-    t_v, slots_v, count_v, panels_v, table_v, table, dense, pred, heads, panel, half, near, far,
+    t_hbm, slots_hbm, count_hbm, mixed_hbm, out_ref,
+    t_v, slots_v, count_v, table_v, table, dense, pred, heads, panel, half, near, far,
     part, sent, got, share, land, share_b, land_b, share_c, land_c, last, fin,
     in_sem,
     s_head, r_head, s_z, r_z, s_xy, r_xy, s_lc, r_lc, s_pair, r_pair, s_line, r_line, s_core, r_core,
@@ -86,11 +86,10 @@
     loads = [
         pltpu.make_async_copy(src, dst, in_sem.at[i])
         for i, (src, dst) in enumerate((
-            (last_hbm, panels_v.at[0]), (prev_hbm, panels_v.at[1]), (older_hbm, panels_v.at[2]),
-            (slots_hbm, slots_v), (count_hbm, count_v), (t_hbm, t_v),
+            (mixed_hbm, pred), (slots_hbm, slots_v), (count_hbm, count_v), (t_hbm, t_v),
         ))
     ]
-    for copy in loads[:3]:
+    for copy in loads[:1]:
         copy.start()
 
     barrier = pltpu.get_barrier_semaphore()
@@ -113,12 +112,8 @@
     for dev in peers:
         greet(dev)
 
-    for copy in loads[:3]:
-        copy.wait()
-    panels = [panels_v[i].astype(F32) for i in range(3)]
-    mixed = 2.5 * panels[0] - 2.0 * panels[1] + 0.5 * panels[2]
-    packed = jnp.concatenate([mixed[:, j * LW : (j + 1) * LW] for j in range(NJ)], axis=0).astype(BF16)
-    pred[...] = packed
+    loads[0].wait()
+    packed = pred[...]
     @pl.when(own_head)
     def _():
         heads[head_slot] = packed
@@ -137,11 +132,11 @@
     def _():
         head_copy(0).start()
 
-    for copy in loads[3:]:
+    for copy in loads[1:]:
         copy.start()
 
-    loads[3].wait()
-    loads[4].wait()
+    loads[1].wait()
+    loads[2].wait()
     key = slots_v[0, 1] * NBLK + slots_v[0, 2]
     slot = lax.broadcasted_iota(jnp.int32, (SLOTS, SLOTS), 1)
     hit = lax.broadcasted_iota(jnp.int32, (SLOTS, SLOTS), 0) == key
@@ -150,10 +145,10 @@
     live = jnp.sum(jnp.where(used, 1, 0), axis=1, keepdims=True)
     table_v[0] = jnp.broadcast_to(inv, (SLOTS, BLK))
     table_v[1] = jnp.broadcast_to(live, (SLOTS, BLK))
-    copy = pltpu.make_async_copy(table_v, table, in_sem.at[6])
+    copy = pltpu.make_async_copy(table_v, table, in_sem.at[4])
     copy.start()
     copy.wait()
-    loads[5].wait()
+    loads[3].wait()
     for u in range(ROWS // BLK):
         for v in range(NBLK):
             k = u * NBLK + v
@@ -399,19 +394,22 @@
 
 
 def local(three_centre, slot_index, slot_count, panel_last, panel_prev, panel_older):
+    mixed = (
+        2.5 * panel_last.astype(F32) - 2.0 * panel_prev.astype(F32) + 0.5 * panel_older.astype(F32)
+    ).astype(BF16)
+    mixed = jnp.transpose(mixed.reshape(4, NJ, LW), (1, 0, 2)).reshape(16, BLK)
     slots = jnp.transpose(slot_index, (0, 3, 1, 2))
     dma = pltpu.SemaphoreType.DMA
     hbm, vmem = pl.BlockSpec(memory_space=pltpu.HBM), pl.BlockSpec(memory_space=pltpu.VMEM)
     out = pl.pallas_call(
         kernel,
         out_shape=jax.ShapeDtypeStruct((4, NBLK * BLK), F32),
-        in_specs=[hbm] * 6,
+        in_specs=[hbm] * 4,
         out_specs=vmem,
         scratch_shapes=[
             pltpu.VMEM((SLOTS, RB, BLK, BLK), BF16),
             pltpu.VMEM((1, 3, 1, SLOTS), jnp.int32),
             pltpu.VMEM((1, 1), jnp.int32),
-            pltpu.VMEM((3, 4, OCC), BF16),
             pltpu.VMEM((2, SLOTS, BLK), jnp.int32),
             pltpu.SMEM((2, SLOTS, BLK), jnp.int32),
             pltpu.VMEM((RB * ROWS, NBLK * BLK), BF16),
@@ -451,7 +449,7 @@
             collective_id=0, has_side_effects=True, vmem_limit_bytes=60 * 1024 * 1024
         ),
         cost_estimate=pl.CostEstimate(flops=2 << 30, bytes_accessed=3 << 20, transcendentals=0),
-    )(three_centre[0, 0], slots, slot_count, panel_last, panel_prev, panel_older)
+    )(three_centre[0, 0], slots, slot_count, mixed)
     return out[None, None]
 
 

time: 74.9 us -> 76.2 us (1.017)
  other arithmetic: 0 us -> 1.32 us
    convert_element_type x0 -> x1, other arithmetic: none -> 1.32 us  [local(): mixed = (2.5 * panel_last.astype(F32) - 2.0 * panel_prev.astype(F32) + 0....]
where the time goes in v7:
time: 76.2 us; the launch traced here: 76 us
  Pallas kernels  72.6 us (95%)
  local copies, waits for them, and re-layouts  1.38 us (2%)
  other arithmetic  1.32 us (2%)
    pallas_call x1, Pallas kernels, local(): pl.pallas_call(kernel, out_shape=jax.ShapeDtypeStruct((4, NBLK * BLK), F3...  72.6 us

profile of v7, /device:TPU:1, one launch (start us, length us, event | category | flops | bytes accessed | tf_op | source)
XLA Modules:
  0.0 76.0 jit_solution(16117353802436331157)
XLA Ops:
  0.7 1.3 %add_convert_fusion = bf16[4,512]{1,0:T(4,128)(2,1)} fusion(bf16[4,512]{1,0:T(4,128)(2,1)} %param.11, bf16[4,512]{1,0:T(4,128)(2,1)} %param.10, bf16[4,512]{1,0:T(4,128)(2,1)} %param.9), kind=kLoop, calls=%fused_computation | loop fusion | flops 18432 | bytes 16384 | tf_op jit(solution)/shard_map/convert_element_type | solution.py:399
  2.0 72.6 %shard_map.64 = f32[4,2048]{1,0:T(4,128)} custom-call(bf16[32,2,128,128]{3,2,1,0:T(8,128)(2,1)} %bitcast.10, s32[1,3,1,32]{3,2,1,0:T(1,128)} %bitcast.11, s32[1,1]{1,0:T(1,128)S(6)} %copy.9.count_hbm, bf16[16,128]{1,0:T(8,128)(2,1)} %bitcast.9), custom_call_target="tpu_custom_call" | custom-call | flops 2147483648 | bytes 3145728 | tf_op jit(solution)/shard_map/pallas_call | solution.py:404
  74.6 1.4 %copy.10 = f32[1,1,4,2048]{3,2,1,0:T(4,128)} copy(f32[1,1,4,2048]{3,2,1,0:T(4,128)} %bitcast.8) | data formatting | bytes 65536
